TPU v7x, 32 devices: a whole 2x2x4 slice. The times are simulated.
32 devices in a mesh: dp: 8 (over z, core), mp: 4 (over y, x).
Axes of the slice: x: 2, y: 2, z: 4, core: 2. Of those that a mesh axis runs over, the one named last changes fastest.
Arguments:
- images_small: bfloat16 [8, 10, 10, 1024], P('dp', None, None, 'mp'), may hold values from -48 to 48
- images_medium: bfloat16 [48, 12, 12, 1024], P('dp', None, None, 'mp'), may hold values from -48 to 48
- images_large: bfloat16 [32, 14, 14, 1024], P('dp', None, None, 'mp'), may hold values from -48 to 48
- width_choice: int32 [3], replicated, may hold values from 0 to 2, each once
- gates_small: int32 [8], P('dp'), may hold values from 0 to 1, as said below
- gates_medium: int32 [48], P('dp'), may hold values from 0 to 1, as said below
- gates_large: int32 [32], P('dp'), may hold values from 0 to 1, as said below
- cotangent_small: bfloat16 [8, 5, 5, 2048], P('dp', None, None, 'mp'), may hold values from -6 to 6
- cotangent_medium: bfloat16 [48, 6, 6, 2048], P('dp', None, None, 'mp'), may hold values from -6 to 6
- cotangent_large: bfloat16 [32, 7, 7, 2048], P('dp', None, None, 'mp'), may hold values from -6 to 6
- squeeze_one: bfloat16 [512, 1024], P('mp'), may hold values from -0.1875 to 0.1875
- squeeze_gain_one: float32 [512], P('mp'), may hold values from 0.25 to 1.75
- squeeze_offset_one: float32 [512], P('mp'), may hold values from -1.2 to 1.2
- spatial_one: bfloat16 [512, 3, 3, 512], P('mp'), may hold values from -0.09375 to 0.09375
- spatial_gain_one: float32 [512], P('mp'), may hold values from 0.25 to 1.75
- spatial_offset_one: float32 [512], P('mp'), may hold values from -1.2 to 1.2
- expand_one: bfloat16 [512, 2048], P('mp'), may hold values from -0.25 to 0.25
- expand_gain_one: float32 [2048], P('mp'), may hold values from 0.25 to 1.75
- expand_offset_one: float32 [2048], P('mp'), may hold values from -1.2 to 1.2
- shortcut_one: bfloat16 [1024, 2048], P('mp'), may hold values from -0.1875 to 0.1875
- shortcut_gain: float32 [2048], P('mp'), may hold values from 0.25 to 1.75
- shortcut_offset: float32 [2048], P('mp'), may hold values from -1.2 to 1.2
- squeeze_two: bfloat16 [512, 2048], P('mp'), may hold values from -0.125 to 0.125
- squeeze_gain_two: float32 [512], P('mp'), may hold values from 0.25 to 1.75
- squeeze_offset_two: float32 [512], P('mp'), may hold values from -1.2 to 1.2
- spatial_two: bfloat16 [512, 3, 3, 512], P('mp'), may hold values from -0.09375 to 0.09375
- spatial_gain_two: float32 [512], P('mp'), may hold values from 0.25 to 1.75
- spatial_offset_two: float32 [512], P('mp'), may hold values from -1.2 to 1.2
- expand_two: bfloat16 [512, 2048], P('mp'), may hold values from -0.25 to 0.25
- expand_gain_two: float32 [2048], P('mp'), may hold values from 0.25 to 1.75
- expand_offset_two: float32 [2048], P('mp'), may hold values from -1.2 to 1.2
Outputs:
- output_small: float32 [8, 5, 5, 2048], P('dp', None, None, 'mp')
- output_medium: float32 [48, 6, 6, 2048], P('dp', None, None, 'mp')
- output_large: float32 [32, 7, 7, 2048], P('dp', None, None, 'mp')
- input_grad_small: float32 [8, 10, 10, 1024], P('dp', None, None, 'mp')
- input_grad_medium: float32 [48, 12, 12, 1024], P('dp', None, None, 'mp')
- input_grad_large: float32 [32, 14, 14, 1024], P('dp', None, None, 'mp')
- grad_squeeze_one: float32 [512, 1024], P('mp')
- grad_squeeze_gain_one: float32 [512], P('mp')
- grad_squeeze_offset_one: float32 [512], P('mp')
- grad_spatial_one: float32 [512, 3, 3, 512], P('mp')
- grad_spatial_gain_one: float32 [512], P('mp')
- grad_spatial_offset_one: float32 [512], P('mp')
- grad_expand_one: float32 [512, 2048], P('mp')
- grad_expand_gain_one: float32 [2048], P('mp')
- grad_expand_offset_one: float32 [2048], P('mp')
- grad_shortcut_one: float32 [1024, 2048], P('mp')
- grad_shortcut_gain: float32 [2048], P('mp')
- grad_shortcut_offset: float32 [2048], P('mp')
- grad_squeeze_two: float32 [512, 2048], P('mp')
- grad_squeeze_gain_two: float32 [512], P('mp')
- grad_squeeze_offset_two: float32 [512], P('mp')
- grad_spatial_two: float32 [512, 3, 3, 512], P('mp')
- grad_spatial_gain_two: float32 [512], P('mp')
- grad_spatial_offset_two: float32 [512], P('mp')
- grad_expand_two: float32 [512, 2048], P('mp')
- grad_expand_gain_two: float32 [2048], P('mp')
- grad_expand_offset_two: float32 [2048], P('mp')
Inputs may be any that keep to these rules, and one draw needn't show every extreme that they name: The three groups take three different widths; group g uses the first 512 * (2 + width_choice[g]) // 4 bottleneck channels. `gates_small`: 1 applies the second block's residual branch to that image; exactly 6 of the images have 1. `gates_medium`: 1 applies the second block's residual branch to that image; exactly 36 of the images have 1. `gates_large`: 1 applies the second block's residual branch to that image; exactly 24 of the images have 1.
All inputs are finite; a program needn't handle non-finite values.
Results may differ from a plain program's by a relative error of at most 0.034.
Values may be sent and summed in bfloat16 or wider, within the bound.
A program may use at most 192 MiB of HBM per device.

v0:
```python
import functools
import types

import jax
import jax.numpy as jnp
import numpy as np
from jax import lax
from jax.experimental import pallas as pl
from jax.experimental.pallas import tpu as pltpu
from jax.sharding import PartitionSpec as P

EPSILON = 1e-05


def sigmoid_linear(values):
    return values * jax.nn.sigmoid(values)


def sigmoid_slope(values):
    logistic = jax.nn.sigmoid(values)
    return logistic * (1.0 + values * (1.0 - logistic))


def pointwise(hidden, weight):
    return jnp.einsum("nhwc,cd->nhwd", hidden, weight, preferred_element_type=jnp.float32)


def back_pointwise(gradients, weight):
    return jnp.einsum("nhwd,cd->nhwc", gradients, weight, preferred_element_type=jnp.float32)


def weight_term(activations, gradients):
    return jnp.einsum("nhwc,nhwd->cd", activations, gradients, preferred_element_type=jnp.float32)


def reduce_pointwise(hidden, weight):
    return jnp.einsum("nhwc,dc->nhwd", hidden, weight, preferred_element_type=jnp.float32)


def reduce_back(gradients, weight):
    return jnp.einsum("nhwd,dc->nhwc", gradients, weight, preferred_element_type=jnp.float32)


def reduce_term(gradients, activations):
    return jnp.einsum("nhwd,nhwc->dc", gradients, activations, preferred_element_type=jnp.float32)


def gather_taps(hidden, stride):
    extent = hidden.shape[1] // stride
    span_end = stride * (extent - 1) + 1
    padded = jnp.pad(hidden, ((0, 0), (1, 1), (1, 1), (0, 0)))
    pieces = [
        padded[:, vertical : vertical + span_end : stride, lateral : lateral + span_end : stride, :]
        for vertical in range(3)
        for lateral in range(3)
    ]
    return jnp.concatenate(pieces, axis=3)


def spread_taps(columns, stride, edge_size, channels):
    extent = columns.shape[1]
    span_end = stride * (extent - 1) + 1
    padded = jnp.zeros((columns.shape[0], edge_size + 2, edge_size + 2, channels), jnp.float32)
    for position in range(9):
        vertical = position // 3
        lateral = position % 3
        padded = padded.at[
            :, vertical : vertical + span_end : stride, lateral : lateral + span_end : stride, :
        ].add(columns[..., position * channels : (position + 1) * channels])
    return padded[:, 1:-1, 1:-1, :]


def stat_terms(values):
    return jnp.stack([jnp.sum(values, axis=(0, 1, 2)), jnp.sum(values * values, axis=(0, 1, 2))])


def grad_terms(gradients, normed):
    return jnp.stack(
        [jnp.sum(gradients, axis=(0, 1, 2)), jnp.sum(gradients * normed, axis=(0, 1, 2))]
    )


def samples_of(values):
    return values.shape[0] * values.shape[1] * values.shape[2] * lax.axis_size("dp")


def norm_apply(values, totals, samples, norm_gain, offset):
    centre = totals[0] / samples
    spread = totals[1] / samples - centre * centre
    factor = lax.rsqrt(spread + EPSILON)
    normed = (values - centre) * factor
    return (normed, factor, normed * norm_gain + offset)


def norm_back(gradients, normed, factor, totals, samples, norm_gain):
    return norm_gain * factor * (gradients - totals[0] / samples - normed * (totals[1] / samples))


def forward_totals(partials):
    return lax.psum(jnp.stack(partials), "dp")


def backward_totals(partials):
    return lax.psum(jnp.stack(partials), "dp")


def gather_channels(pieces):
    return (
        lax.all_gather(pieces[0], "mp", axis=3, tiled=True),
        lax.all_gather(pieces[1], "mp", axis=3, tiled=True),
        lax.all_gather(pieces[2], "mp", axis=3, tiled=True),
    )


def gather_hidden(pieces):
    return (
        lax.all_gather(pieces[0], "mp", axis=3, tiled=True),
        lax.all_gather(pieces[1], "mp", axis=3, tiled=True),
        lax.all_gather(pieces[2], "mp", axis=3, tiled=True),
    )


def gather_spatial_grads(pieces):
    return (
        lax.all_gather(pieces[0], "mp", axis=3, tiled=True),
        lax.all_gather(pieces[1], "mp", axis=3, tiled=True),
        lax.all_gather(pieces[2], "mp", axis=3, tiled=True),
    )


def gather_entry_grads(pieces):
    return (
        lax.all_gather(pieces[0], "mp", axis=3, tiled=True),
        lax.all_gather(pieces[1], "mp", axis=3, tiled=True),
        lax.all_gather(pieces[2], "mp", axis=3, tiled=True),
    )


def front_forward(gathered, stride, params, width_masks):
    squeeze, squeeze_gain, squeeze_offset, spatial_conv, spatial_gain, spatial_offset = params
    entry = [reduce_pointwise(values, squeeze) for values in gathered]
    entry_totals = forward_totals([stat_terms(values) for values in entry])
    entry_norm = [
        norm_apply(
            entry[member],
            entry_totals[member],
            samples_of(entry[member]),
            squeeze_gain,
            squeeze_offset,
        )
        for member in range(3)
    ]
    hidden = [
        (width_masks[member] * sigmoid_linear(entry_norm[member][2])).astype(jnp.bfloat16)
        for member in range(3)
    ]
    hidden_full = gather_hidden(hidden)
    taps = [gather_taps(values, stride) for values in hidden_full]
    spatial_rows = spatial_conv.reshape(spatial_conv.shape[0], -1)
    middle = [reduce_pointwise(values, spatial_rows) for values in taps]
    middle_totals = forward_totals([stat_terms(values) for values in middle])
    middle_norm = [
        norm_apply(
            middle[member],
            middle_totals[member],
            samples_of(middle[member]),
            spatial_gain,
            spatial_offset,
        )
        for member in range(3)
    ]
    narrow = [
        (width_masks[member] * sigmoid_linear(middle_norm[member][2])).astype(jnp.bfloat16)
        for member in range(3)
    ]
    return (entry_norm, taps, middle_norm, narrow)


def front_backward(narrow_grads, saved, gathered, stride, params, width_masks, column_weights):
    squeeze, squeeze_gain, squeeze_offset, spatial_conv, spatial_gain, spatial_offset = params
    entry_norm, taps, middle_norm, narrow = saved
    middle_out = [
        narrow_grads[member] * width_masks[member] * sigmoid_slope(middle_norm[member][2])
        for member in range(3)
    ]
    middle_totals = backward_totals(
        [grad_terms(middle_out[member], middle_norm[member][0]) for member in range(3)]
    )
    middle_grads = [
        norm_back(
            middle_out[member],
            middle_norm[member][0],
            middle_norm[member][1],
            middle_totals[member],
            samples_of(middle_out[member]),
            spatial_gain,
        ).astype(jnp.bfloat16)
        for member in range(3)
    ]
    spatial_grad = sum(
        (reduce_term(middle_grads[member], taps[member]) for member in range(3))
    ).reshape(spatial_conv.shape)
    squeeze_cols, spatial_cols = column_weights
    channels = spatial_cols.shape[3]
    spatial_flat = spatial_cols.reshape(spatial_cols.shape[0], -1)
    middle_full = gather_spatial_grads(middle_grads)
    hidden_grads = [
        spread_taps(
            reduce_back(middle_full[member], spatial_flat),
            stride,
            gathered[member].shape[1],
            channels,
        )
        for member in range(3)
    ]
    entry_out = [
        hidden_grads[member] * width_masks[member] * sigmoid_slope(entry_norm[member][2])
        for member in range(3)
    ]
    entry_totals = backward_totals(
        [grad_terms(entry_out[member], entry_norm[member][0]) for member in range(3)]
    )
    entry_grads = [
        norm_back(
            entry_out[member],
            entry_norm[member][0],
            entry_norm[member][1],
            entry_totals[member],
            samples_of(entry_out[member]),
            squeeze_gain,
        ).astype(jnp.bfloat16)
        for member in range(3)
    ]
    squeeze_grad = sum((reduce_term(entry_grads[member], gathered[member]) for member in range(3)))
    entry_full = gather_entry_grads(entry_grads)
    squeeze_flat = squeeze_cols.reshape(squeeze_cols.shape[0], -1)
    input_part = [reduce_back(entry_full[member], squeeze_flat) for member in range(3)]
    gain_grads = (
        jnp.sum(entry_totals[:, 1], axis=0),
        jnp.sum(entry_totals[:, 0], axis=0),
        jnp.sum(middle_totals[:, 1], axis=0),
        jnp.sum(middle_totals[:, 0], axis=0),
    )
    return (input_part, squeeze_grad, spatial_grad, gain_grads)


def tail_forward(narrow, bypass_inputs, expand, shortcut):
    partials = []
    for member in range(3):
        pieces = [pointwise(narrow[member], expand)]
        if shortcut is not None:
            pieces.append(pointwise(bypass_inputs[member], shortcut))
        partials.append(jnp.stack(pieces))
    partials = (
        lax.psum_scatter(
            partials[0].astype(jnp.bfloat16), "mp", scatter_dimension=4, tiled=True
        ).astype(jnp.float32),
        lax.psum_scatter(
            partials[1].astype(jnp.bfloat16), "mp", scatter_dimension=4, tiled=True
        ).astype(jnp.float32),
        lax.psum_scatter(
            partials[2].astype(jnp.bfloat16), "mp", scatter_dimension=4, tiled=True
        ).astype(jnp.float32),
    )
    return (partials, narrow)


def tail_backward(gradients, sources, bypass_inputs, expand, shortcut):
    arriving = (
        lax.all_gather(gradients[0], "mp", axis=4, tiled=True),
        lax.all_gather(gradients[1], "mp", axis=4, tiled=True),
        lax.all_gather(gradients[2], "mp", axis=4, tiled=True),
    )
    expand_grad = sum((weight_term(sources[member], arriving[member][0]) for member in range(3)))
    narrow_terms = [back_pointwise(arriving[member][0], expand) for member in range(3)]
    if shortcut is None:
        return (narrow_terms, expand_grad, None, None)
    shortcut_grad = sum(
        (weight_term(bypass_inputs[member], arriving[member][1]) for member in range(3))
    )
    bypass_terms = [back_pointwise(arriving[member][1], shortcut) for member in range(3)]
    return (narrow_terms, expand_grad, shortcut_grad, bypass_terms)


def on_device(
    images_small,
    images_medium,
    images_large,
    width_choice,
    gates_small,
    gates_medium,
    gates_large,
    cotangent_small,
    cotangent_medium,
    cotangent_large,
    squeeze_one,
    squeeze_gain_one,
    squeeze_offset_one,
    spatial_one,
    spatial_gain_one,
    spatial_offset_one,
    expand_one,
    expand_gain_one,
    expand_offset_one,
    shortcut_one,
    shortcut_gain,
    shortcut_offset,
    squeeze_two,
    squeeze_gain_two,
    squeeze_offset_two,
    spatial_two,
    spatial_gain_two,
    spatial_offset_two,
    expand_two,
    expand_gain_two,
    expand_offset_two,
):
    images = [images_small, images_medium, images_large]
    depth_gates = [
        flags.astype(jnp.float32)[:, None, None, None]
        for flags in (gates_small, gates_medium, gates_large)
    ]
    cotangents = [
        values.astype(jnp.float32)
        for values in (cotangent_small, cotangent_medium, cotangent_large)
    ]
    mid_local = squeeze_one.shape[0]
    channel_index = lax.axis_index("mp") * mid_local + jnp.arange(mid_local, dtype=jnp.int32)
    limits = mid_local * lax.axis_size("mp") * (2 + width_choice) // 4
    width_masks = [(channel_index < limits[member]).astype(jnp.float32) for member in range(3)]
    out_local = expand_gain_one.shape[0]
    params_one = (
        squeeze_one,
        squeeze_gain_one,
        squeeze_offset_one,
        spatial_one,
        spatial_gain_one,
        spatial_offset_one,
    )
    params_two = (
        squeeze_two,
        squeeze_gain_two,
        squeeze_offset_two,
        spatial_two,
        spatial_gain_two,
        spatial_offset_two,
    )
    expand_first, bypass_weight, expand_second = (expand_one, shortcut_one, expand_two)
    squeeze_cols_one, spatial_cols_one, squeeze_cols_two, spatial_cols_two = (
        lax.all_to_all(
            squeeze_one.reshape(mid_local, 1, 1, -1), "mp", split_axis=3, concat_axis=0, tiled=True
        ),
        lax.all_to_all(spatial_one, "mp", split_axis=3, concat_axis=0, tiled=True),
        lax.all_to_all(
            squeeze_two.reshape(mid_local, 1, 1, -1), "mp", split_axis=3, concat_axis=0, tiled=True
        ),
        lax.all_to_all(spatial_two, "mp", split_axis=3, concat_axis=0, tiled=True),
    )
    columns_one = (squeeze_cols_one, spatial_cols_one)
    columns_two = (squeeze_cols_two, spatial_cols_two)
    first_full = gather_channels(images)
    first_saved = front_forward(first_full, 2, params_one, width_masks)
    bypass_inputs = [values[:, ::2, ::2, :] for values in images]
    first_tail, first_sources = tail_forward(
        first_saved[3], bypass_inputs, expand_first, bypass_weight
    )
    first_totals = forward_totals(
        [
            jnp.concatenate(
                [stat_terms(first_tail[member][0]), stat_terms(first_tail[member][1])], axis=1
            )
            for member in range(3)
        ]
    )
    widened_norm = [
        norm_apply(
            first_tail[member][0],
            first_totals[member][:, :out_local],
            samples_of(first_tail[member][0]),
            expand_gain_one,
            expand_offset_one,
        )
        for member in range(3)
    ]
    bypass_norm = [
        norm_apply(
            first_tail[member][1],
            first_totals[member][:, out_local:],
            samples_of(first_tail[member][1]),
            shortcut_gain,
            shortcut_offset,
        )
        for member in range(3)
    ]
    first_sum = [widened_norm[member][2] + bypass_norm[member][2] for member in range(3)]
    block_out = [sigmoid_linear(values) for values in first_sum]
    second_full = gather_channels([values.astype(jnp.bfloat16) for values in block_out])
    second_saved = front_forward(second_full, 1, params_two, width_masks)
    second_tail, second_sources = tail_forward(second_saved[3], None, expand_second, None)
    second_totals = forward_totals([stat_terms(second_tail[member][0]) for member in range(3)])
    final_norm = [
        norm_apply(
            second_tail[member][0],
            second_totals[member],
            samples_of(second_tail[member][0]),
            expand_gain_two,
            expand_offset_two,
        )
        for member in range(3)
    ]
    second_sum = [
        block_out[member] + depth_gates[member] * final_norm[member][2] for member in range(3)
    ]
    results = [sigmoid_linear(values) for values in second_sum]
    second_slope = [sigmoid_slope(second_sum[member]) * cotangents[member] for member in range(3)]
    final_out = [depth_gates[member] * second_slope[member] for member in range(3)]
    final_totals = backward_totals(
        [grad_terms(final_out[member], final_norm[member][0]) for member in range(3)]
    )
    final_grads = [
        norm_back(
            final_out[member],
            final_norm[member][0],
            final_norm[member][1],
            final_totals[member],
            samples_of(final_out[member]),
            expand_gain_two,
        ).astype(jnp.bfloat16)[None]
        for member in range(3)
    ]
    second_result = tail_backward(final_grads, second_sources, None, expand_second, None)
    second_input_part, squeeze_two_grad, spatial_two_grad, second_gain_grads = front_backward(
        second_result[0], second_saved, second_full, 1, params_two, width_masks, columns_two
    )
    expand_two_grad = second_result[1]
    block_grads = [second_slope[member] + second_input_part[member] for member in range(3)]
    first_slope = [sigmoid_slope(first_sum[member]) * block_grads[member] for member in range(3)]
    first_grad_totals = backward_totals(
        [
            jnp.concatenate(
                [
                    grad_terms(first_slope[member], widened_norm[member][0]),
                    grad_terms(first_slope[member], bypass_norm[member][0]),
                ],
                axis=1,
            )
            for member in range(3)
        ]
    )
    tail_grads = [
        jnp.stack(
            [
                norm_back(
                    first_slope[member],
                    widened_norm[member][0],
                    widened_norm[member][1],
                    first_grad_totals[member][:, :out_local],
                    samples_of(first_slope[member]),
                    expand_gain_one,
                ),
                norm_back(
                    first_slope[member],
                    bypass_norm[member][0],
                    bypass_norm[member][1],
                    first_grad_totals[member][:, out_local:],
                    samples_of(first_slope[member]),
                    shortcut_gain,
                ),
            ]
        ).astype(jnp.bfloat16)
        for member in range(3)
    ]
    first_result = tail_backward(
        tail_grads, first_sources, bypass_inputs, expand_first, bypass_weight
    )
    expand_one_grad = first_result[1]
    shortcut_grad = first_result[2]
    bypass_terms = first_result[3]
    first_input_part, squeeze_one_grad, spatial_one_grad, first_gain_grads = front_backward(
        first_result[0], first_saved, first_full, 2, params_one, width_masks, columns_one
    )
    input_grads = [
        first_input_part[member].at[:, ::2, ::2, :].add(bypass_terms[member]) for member in range(3)
    ]
    summed = (
        lax.psum(squeeze_one_grad.astype(jnp.bfloat16), "dp").astype(jnp.float32),
        lax.psum(spatial_one_grad.astype(jnp.bfloat16), "dp").astype(jnp.float32),
        lax.psum(expand_one_grad.astype(jnp.bfloat16), "dp").astype(jnp.float32),
        lax.psum(shortcut_grad.astype(jnp.bfloat16), "dp").astype(jnp.float32),
        lax.psum(squeeze_two_grad.astype(jnp.bfloat16), "dp").astype(jnp.float32),
        lax.psum(spatial_two_grad.astype(jnp.bfloat16), "dp").astype(jnp.float32),
        lax.psum(expand_two_grad.astype(jnp.bfloat16), "dp").astype(jnp.float32),
    )
    expand_gain_one_grad = jnp.sum(first_grad_totals[:, 1, :out_local], axis=0)
    expand_offset_one_grad = jnp.sum(first_grad_totals[:, 0, :out_local], axis=0)
    shortcut_gain_grad = jnp.sum(first_grad_totals[:, 1, out_local:], axis=0)
    shortcut_offset_grad = jnp.sum(first_grad_totals[:, 0, out_local:], axis=0)
    expand_gain_two_grad = jnp.sum(final_totals[:, 1], axis=0)
    expand_offset_two_grad = jnp.sum(final_totals[:, 0], axis=0)
    return (
        results[0],
        results[1],
        results[2],
        input_grads[0],
        input_grads[1],
        input_grads[2],
        summed[0],
        first_gain_grads[0],
        first_gain_grads[1],
        summed[1],
        first_gain_grads[2],
        first_gain_grads[3],
        summed[2],
        expand_gain_one_grad,
        expand_offset_one_grad,
        summed[3],
        shortcut_gain_grad,
        shortcut_offset_grad,
        summed[4],
        second_gain_grads[0],
        second_gain_grads[1],
        summed[5],
        second_gain_grads[2],
        second_gain_grads[3],
        summed[6],
        expand_gain_two_grad,
        expand_offset_two_grad,
    )


LANE = 128
GUARD = 32
MESH_ID = pl.DeviceIdType.MESH
DMA = pltpu.SemaphoreType.DMA
VMEM = pltpu.VMEM
F32 = jnp.float32
BF16 = jnp.bfloat16
WEIGHTS = 7
TENSOR_Q1, TENSOR_S1, TENSOR_E1, TENSOR_SC, TENSOR_Q2, TENSOR_S2, TENSOR_E2 = range(WEIGHTS)
NORM_Q1, NORM_S1, NORM_Q2, NORM_S2 = range(4)
NORM_E1, NORM_SC, NORM_E2 = range(3)


def nn(left, right):
    return lax.dot_general(left, right, (((1,), (0,)), ((), ())), preferred_element_type=F32)


def nt(left, right):
    return lax.dot_general(left, right, (((1,), (1,)), ((), ())), preferred_element_type=F32)


def tn(left, right):
    return lax.dot_general(left, right, (((0,), (0,)), ((), ())), preferred_element_type=F32)


def bag(tree):
    if isinstance(tree, dict):
        return types.SimpleNamespace(**{name: bag(value) for name, value in tree.items()})
    return tree


class Segment:
    def __init__(self, group, start, images, side, replicas):
        self.group = group
        self.side = side
        self.images = images
        self.inside = images <= 4
        self.right = images if self.inside else 1
        self.down = self.right * side
        self.start = start
        self.real = images * side * side
        self.size = -(-self.real // 16) * 16
        self.stop = start + self.size
        self.count = float(self.real * replicas)

    def pixel_first(self, values):
        return values.transpose(1, 2, 0, 3) if self.inside else values

    def image_first(self, values):
        return values.transpose(2, 0, 1, 3) if self.inside else values


class Chain:
    def __init__(self, groups, shapes, replicas):
        self.segments = []
        start = 0
        for group in groups:
            images, side = shapes[group]
            segment = Segment(group, start, images, side // 2, replicas)
            self.segments.append(segment)
            start = segment.stop
        self.rows = start
        self.padded = start + 2 * GUARD


class Weight:
    def __init__(self, block, width, taps, direct):
        self.block = block
        self.width = width
        self.taps = taps
        self.direct = direct
        self.ways = 4 if direct else 2
        self.piece = block // (2 * self.ways)


def weight_table(mid, wide, inner):
    return [
        Weight(mid, inner, 1, True),
        Weight(mid, mid, 9, True),
        Weight(mid, wide, 1, False),
        Weight(inner, wide, 1, True),
        Weight(mid, wide, 1, False),
        Weight(mid, mid, 9, True),
        Weight(mid, wide, 1, False),
    ]


def chain_scratch(chain, mid, wide, inner, dpn, mpn):
    rows = chain.rows
    padded = chain.padded
    near = mpn - 1

    def summed(lead, width):
        return dict(
            send=VMEM((mpn, lead, width), BF16),
            recv=VMEM((near, lead, width), BF16),
            sent=DMA((near,)),
            came=DMA((near,)),
        )

    def gathered(lead, width):
        return dict(full=VMEM((mpn, lead, width), BF16), sent=DMA((near,)), came=DMA((near,)))

    def reduced(terms, width):
        depth = -(-(len(chain.segments) * terms * width // LANE) // 8) * 8
        return dict(
            stat=VMEM((dpn, depth, LANE), F32), sent=DMA((dpn - 1,)), came=DMA((dpn,))
        )

    return dict(
        z1=summed(4 * rows, mid),
        z2=summed(rows, mid),
        u1=summed(rows, mid),
        u2=summed(rows, mid),
        b2=summed(rows, mid),
        b1=summed(rows, mid),
        bx=summed(rows, inner),
        xs=gathered(rows, inner),
        h2=gathered(rows, mid),
        v2=gathered(rows, mid),
        g2=gathered(rows, mid),
        g1=gathered(rows, mid),
        k2=gathered(rows, mid),
        k1=gathered(4 * rows, mid),
        f1=reduced(2, mid),
        f2=reduced(2, mid),
        f3=reduced(2, wide),
        fp=reduced(2, wide),
        f4=reduced(2, mid),
        f5=reduced(2, mid),
        f6=reduced(2, wide),
        r6=reduced(2, wide),
        r5=reduced(2, mid),
        r4=reduced(2, mid),
        r3=reduced(3, wide),
        r2=reduced(2, mid),
        r1=reduced(2, mid),
        n1=VMEM((4, rows, mid), F32),
        sl1=VMEM((4, rows, mid), F32),
        h1=VMEM((4, padded, mid), F32),
        t1=VMEM((rows, 9 * mid), BF16),
        n2=VMEM((rows, mid), F32),
        sl2=VMEM((rows, mid), F32),
        n3=VMEM((rows, wide), F32),
        bypass=VMEM((rows, wide), F32),
        y=VMEM((rows, wide), F32),
        slq=VMEM((rows, wide), F32),
        r=VMEM((rows, wide), BF16),
        n4=VMEM((rows, mid), F32),
        sl4=VMEM((rows, mid), F32),
        v1=VMEM((padded, mid), F32),
        t2=VMEM((rows, 9 * mid), BF16),
        n5=VMEM((rows, mid), F32),
        sl5=VMEM((rows, mid), F32),
        n6=VMEM((rows, wide), F32),
        d2=VMEM((rows, wide), F32),
        du3=VMEM((rows, wide), BF16),
        dz3=VMEM((rows, wide), BF16),
        dzp=VMEM((rows, wide), BF16),
        dt=VMEM((padded, 9 * mid), F32),
        d=VMEM((4, rows, mid), F32),
        back=VMEM((rows, inner), F32),
        gate=VMEM((rows, LANE), F32),
        facm=VMEM((4, 8, mid), F32),
        facw=VMEM((3, 8, wide), F32),
        gm=VMEM((8, mid), F32),
        gw=VMEM((8, wide), F32),
    )


def weight_scratch(weight, dpn, mpn):
    near = mpn - 1
    spread = (mpn, weight.taps, weight.block // 2, weight.width)
    pieces = (weight.ways, mpn, weight.taps, weight.piece, weight.width)
    return dict(
        full=VMEM((weight.taps, mpn * weight.block, weight.width), BF16),
        sent=DMA((near,)),
        came=DMA((near,)),
        passed=DMA((near,)),
        given=DMA((near,)),
        own=DMA((1,)),
        part=VMEM((mpn, weight.taps, weight.block, weight.width), BF16),
        twin=VMEM(spread, BF16),
        sums=VMEM(pieces, BF16),
        hop=VMEM(pieces, BF16),
        fin=VMEM(pieces, BF16),
        swap=VMEM(pieces, BF16),
        twins=DMA((2,)),
        swaps=DMA((2,)),
        outs=DMA((2,)),
        hop_sent=DMA((4,)),
        hop_came=DMA((4,)),
        mix_sent=DMA((near,)),
        mix_came=DMA((near,)),
        cast_sent=DMA((4,)),
        cast_came=DMA((4,)),
    )


class Body:
    def __init__(self, given, made, scratch, chains, weights, sizes):
        self.given = given
        self.made = made
        self.links = scratch.chains
        self.weights = weights
        self.held = scratch.weights
        self.chains = chains
        self.mid, self.wide, self.inner, self.dpn, self.mpn = sizes
        self.dp = lax.axis_index("dp")
        self.mp = lax.axis_index("mp")
        self.z = lax.div(self.dp, 2)
        self.core = lax.rem(self.dp, 2)
        self.levels = self.dpn // 2
        across = lax.div(self.mp, 2)
        along = lax.rem(self.mp, 2)
        self.peers = (
            across * 2 + (1 - along),
            (1 - across) * 2 + along,
            (1 - across) * 2 + (1 - along),
        )
        self.twin = self.z * 2 + (1 - self.core)
        self.others = [lax.rem(self.dp + step, self.dpn) for step in range(1, self.dpn)]
        self.stack = [lax.rem(self.z + step, self.levels) for step in range(1, self.levels)]
        self.flying = {}
        self.passing = {}
        self.present = set()

    def barrier(self):
        semaphore = pltpu.get_barrier_semaphore()
        for peer in self.peers:
            pl.semaphore_signal(
                semaphore, inc=1, device_id=(self.dp, peer), device_id_type=MESH_ID
            )
        for other in self.others:
            pl.semaphore_signal(
                semaphore, inc=1, device_id=(other, self.mp), device_id_type=MESH_ID
            )
        pl.semaphore_wait(semaphore, len(self.peers) + len(self.others))

    def remote(self, source, target, sent, came, device):
        return pltpu.make_async_remote_copy(
            src_ref=source,
            dst_ref=target,
            send_sem=sent,
            recv_sem=came,
            device_id=device,
            device_id_type=MESH_ID,
        )


    def scatter(self, link, values):
        width = link.send.shape[2]
        for block in range(self.mpn):
            link.send[block] = values[:, block * width : (block + 1) * width].astype(BF16)
        copies = []
        for step, peer in enumerate(self.peers):
            copy = self.remote(
                link.send.at[peer],
                link.recv.at[step],
                link.sent.at[step],
                link.came.at[step],
                (self.dp, peer),
            )
            copy.start()
            copies.append(copy)
        yield
        for copy in copies:
            copy.wait()
        total = link.send[self.mp].astype(F32)
        for step in range(self.mpn - 1):
            total = total + link.recv[step].astype(F32)
        return total

    def gather(self, link):
        full = link.full
        copies = []
        for step, peer in enumerate(self.peers):
            copy = self.remote(
                full.at[self.mp],
                full.at[self.mp],
                link.sent.at[step],
                link.came.at[step],
                (self.dp, peer),
            )
            copy.start()
            copies.append(copy)
        yield
        for step, peer in enumerate(self.peers):
            copies[step].wait_send()
            self.remote(
                full.at[peer],
                full.at[peer],
                link.sent.at[step],
                link.came.at[step],
                (self.dp, peer),
            ).wait_recv()

    def joined(self, link):
        return jnp.concatenate([link.full[block] for block in range(self.mpn)], axis=1)

    def reduce(self, link, terms):
        stat = link.stat
        depth = stat.shape[1]
        lanes = terms[0].shape[1] // LANE
        lines = [
            term[:, lane * LANE : (lane + 1) * LANE] for term in terms for lane in range(lanes)
        ]
        if depth > len(lines):
            lines.append(jnp.zeros((depth - len(lines), LANE), F32))
        stat[self.dp] = jnp.concatenate(lines, axis=0)
        copies = []
        for step, other in enumerate(self.others):
            copy = self.remote(
                stat.at[self.dp],
                stat.at[self.dp],
                link.sent.at[step],
                link.came.at[self.dp],
                (other, self.mp),
            )
            copy.start()
            copies.append(copy)
        yield
        for step, other in enumerate(self.others):
            copies[step].wait_send()
            self.remote(
                stat.at[other],
                stat.at[other],
                link.sent.at[step],
                link.came.at[other],
                (other, self.mp),
            ).wait_recv()
        total = stat[0]
        for source in range(1, self.dpn):
            total = total + stat[source]
        rows = []
        for index in range(len(terms)):
            first = index * lanes
            pieces = [total[first + lane : first + lane + 1] for lane in range(lanes)]
            rows.append(pieces[0] if lanes == 1 else jnp.concatenate(pieces, axis=1))
        return rows


    def half(self, block, first, core):
        return pl.ds(pl.multiple_of(first + core * (block // 2), 16), block // 2)

    def weight_start(self, tensor):
        weight = self.weights[tensor]
        held = self.held[tensor]
        source = self.given.weights[tensor]
        block, width = weight.block, weight.width

        def columns(device):
            return pl.ds(pl.multiple_of(device * width, LANE), width)

        copies = []
        for step, peer in enumerate(self.peers):
            copy = self.remote(
                source.at[:, self.half(block, 0, self.core), columns(peer)],
                held.full.at[:, self.half(block, self.mp * block, self.core), :],
                held.sent.at[step],
                held.came.at[step],
                (self.dp, peer),
            )
            copy.start()
            copies.append(copy)
        own = pltpu.make_async_copy(
            source.at[:, :, columns(self.mp)],
            held.full.at[:, pl.ds(pl.multiple_of(self.mp * block, 16), block), :],
            held.own.at[0],
        )
        own.start()
        self.flying[tensor] = (copies, own)

    def weight_pass(self, tensor):
        if tensor in self.passing:
            return
        copies, own = self.flying[tensor]
        block = self.weights[tensor].block
        held = self.held[tensor]
        passed = []
        for step, peer in enumerate(self.peers):
            came = held.full.at[:, self.half(block, peer * block, self.core), :]
            copies[step].wait_send()
            self.remote(
                came, came, held.sent.at[step], held.came.at[step], (self.dp, peer)
            ).wait_recv()
            copy = self.remote(
                came, came, held.passed.at[step], held.given.at[step], (self.twin, self.mp)
            )
            copy.start()
            passed.append(copy)
        own.wait()
        self.passing[tensor] = passed

    def weight(self, tensor):
        held = self.held[tensor]
        weight = self.weights[tensor]
        block = weight.block
        if tensor not in self.present:
            self.weight_pass(tensor)
            for step, peer in enumerate(self.peers):
                rest = held.full.at[:, self.half(block, peer * block, 1 - self.core), :]
                self.passing[tensor][step].wait_send()
                self.remote(
                    rest, rest, held.passed.at[step], held.given.at[step], (self.twin, self.mp)
                ).wait_recv()
            self.present.add(tensor)
        if weight.taps == 1:
            return held.full[0]
        return jnp.concatenate([held.full[tap] for tap in range(weight.taps)], axis=1)


    def keep(self, segment, values):
        if segment.real == segment.size:
            return values
        rows = lax.broadcasted_iota(jnp.int32, values.shape, values.ndim - 2)
        return jnp.where(rows < segment.real, values, 0.0)

    def factors(self, sums, squares, count):
        centre = sums / count
        spread = squares / count - centre * centre
        return centre, lax.rsqrt(spread + EPSILON)

    def sum_rows(self, values):
        return jnp.sum(values.reshape(-1, values.shape[-1]), axis=0, keepdims=True)

    def moments(self, chain, values):
        terms = []
        for segment in chain.segments:
            part = values[..., segment.start : segment.stop, :]
            terms.append(self.sum_rows(part))
            terms.append(self.sum_rows(part * part))
        return terms

    def mid_row(self, norm, what):
        return self.given.mids[norm * 2 + what][...].reshape(1, self.mid)

    def wide_row(self, norm, what):
        return self.given.wides[norm * 2 + what][...].reshape(1, self.wide)

    def width_mask(self, group):
        limit = lax.div(self.mid * self.mpn * (2 + self.given.widths[group]), 4)
        index = lax.broadcasted_iota(jnp.int32, (1, self.mid), 1) + self.mp * self.mid
        return (index < limit).astype(F32)

    def narrow_norm(self, chain, link, norm, values, totals, normed_ref, slope_ref, store):
        gain = self.mid_row(norm, 0)
        offset = self.mid_row(norm, 1)
        for index, segment in enumerate(chain.segments):
            rows = slice(segment.start, segment.stop)
            count = segment.count * (4 if norm == NORM_Q1 else 1)
            centre, factor = self.factors(totals[2 * index], totals[2 * index + 1], count)
            link.facm[norm, index : index + 1, :] = factor
            mask = self.width_mask(segment.group)
            normed = (values[..., rows, :] - centre) * factor
            normed_ref[..., rows, :] = normed
            affine = normed * gain + offset
            logistic = jax.nn.sigmoid(affine)
            slope_ref[..., rows, :] = mask * (logistic * (1.0 + affine * (1.0 - logistic)))
            store(segment, self.keep(segment, mask * (affine * logistic)).astype(BF16))

    def narrow_terms(self, chain, gradients, normed_ref):
        terms = []
        for segment in chain.segments:
            rows = slice(segment.start, segment.stop)
            part = gradients[..., rows, :]
            terms.append(self.sum_rows(part))
            terms.append(self.sum_rows(part * normed_ref[..., rows, :]))
        return terms

    def narrow_back(self, chain, link, norm, gradients_ref, totals, normed_ref, store):
        gain = self.mid_row(norm, 0)
        gain_total = None
        offset_total = None
        for index, segment in enumerate(chain.segments):
            rows = slice(segment.start, segment.stop)
            count = segment.count * (4 if norm == NORM_Q1 else 1)
            factor = link.facm[norm, index : index + 1, :]
            first, second = totals[2 * index], totals[2 * index + 1]
            gain_total = second if gain_total is None else gain_total + second
            offset_total = first if offset_total is None else offset_total + first
            change = (gain * factor) * (
                gradients_ref[..., rows, :]
                - first / count
                - normed_ref[..., rows, :] * (second / count)
            )
            store(segment, self.keep(segment, change).astype(BF16))
        link.gm[2 * norm : 2 * norm + 1, :] = gain_total
        link.gm[2 * norm + 1 : 2 * norm + 2, :] = offset_total


    def edge(self, edges, start, size, down, right):
        mask = None
        for shift, first in ((down, 0), (right, 2)):
            if shift == 0:
                continue
            values = edges[first + (0 if shift < 0 else 1), start : start + size, :]
            mask = values if mask is None else mask * values
        return mask

    def tap_list(self, stride):
        taps = []
        for vertical in range(3):
            for lateral in range(3):
                if stride == 2:
                    plane = 2 * (vertical != 1) + (lateral != 1)
                    taps.append((plane, -(vertical == 0), -(lateral == 0)))
                else:
                    taps.append((0, vertical - 1, lateral - 1))
        return taps

    def collect(self, chain, stride, padded, edges, taps_ref):
        mid = self.mid
        for position, (plane, down, right) in enumerate(self.tap_list(stride)):
            for index, segment in enumerate(chain.segments):
                shift = down * segment.down + right * segment.right
                base = GUARD + segment.start
                rows = slice(base + shift, base + shift + segment.size)
                values = padded[plane, rows, :] if stride == 2 else padded[rows, :]
                mask = self.edge(edges.at[index], base, segment.size, down, right)
                if mask is not None:
                    values = values * mask
                taps_ref[
                    segment.start : segment.stop, position * mid : (position + 1) * mid
                ] = values.astype(BF16)

    def spread(self, chain, stride, columns, edges):
        mid = self.mid
        taps = self.tap_list(stride)
        results = []
        for index, segment in enumerate(chain.segments):
            base = GUARD + segment.start
            for plane in range(4 if stride == 2 else 1):
                total = None
                for position, (where, down, right) in enumerate(taps):
                    if where != plane:
                        continue
                    start = base - (down * segment.down + right * segment.right)
                    values = columns[
                        start : start + segment.size, position * mid : (position + 1) * mid
                    ]
                    mask = self.edge(edges.at[index], start, segment.size, down, right)
                    if mask is not None:
                        values = values * mask
                    total = values if total is None else total + values
                results.append((segment, plane, self.keep(segment, total)))
        return results


    def clear(self, chain, link):
        rows = chain.rows
        for array in (link.h1, link.v1, link.dt):
            blank = jnp.zeros(array.shape[:-2] + (GUARD, array.shape[-1]), array.dtype)
            array[..., 0:GUARD, :] = blank
            array[..., GUARD + rows : 2 * GUARD + rows, :] = blank
        link.gm[...] = jnp.zeros_like(link.gm)
        link.gw[...] = jnp.zeros_like(link.gw)
        for segment in chain.segments:
            flags = [
                self.given.gates[segment.group][image].astype(F32)
                for image in range(segment.images)
            ]
            area = segment.side * segment.side
            link.gate[segment.start : segment.stop, :] = jnp.zeros((segment.size, LANE), F32)
            if segment.inside:
                rows = lax.broadcasted_iota(jnp.int32, (segment.size, LANE), 0)
                place = lax.rem(rows, segment.images)
                total = jnp.zeros((segment.size, LANE), F32)
                for image, flag in enumerate(flags):
                    total = jnp.where(place == image, flag, total)
                link.gate[segment.start : segment.stop, :] = total
            else:
                for image, flag in enumerate(flags):
                    start = segment.start + image * area
                    link.gate[start : start + area, :] = jnp.full((area, LANE), flag, F32)

    def gates(self, link, rows):
        return jnp.concatenate([link.gate[rows, :]] * (self.wide // LANE), axis=1)

    def bypass(self, chain, link, pixels):
        link.xs.full[self.mp] = pixels[0]
        yield from self.gather(link.xs)
        product = nn(self.joined(link.xs), self.weight(TENSOR_SC))
        link.bypass[...] = product
        totals = yield from self.reduce(link.fp, self.moments(chain, product))
        for index, segment in enumerate(chain.segments):
            rows = slice(segment.start, segment.stop)
            centre, factor = self.factors(
                totals[2 * index], totals[2 * index + 1], segment.count
            )
            link.facw[NORM_SC, index : index + 1, :] = factor
            link.bypass[rows, :] = (link.bypass[rows, :] - centre) * factor

    def chain(self, chain, link, given, made):
        rows = chain.rows
        mid = self.mid

        def into(full):
            def store(segment, values):
                full[self.mp, segment.start : segment.stop, :] = values

            return store

        pixels = given.pixels[...].reshape(4 * rows, self.inner)
        total = yield from self.scatter(link.z1, nt(pixels, self.weight(TENSOR_Q1)))
        total = total.reshape(4, rows, mid)
        link.n1[...] = total
        totals = yield from self.reduce(link.f1, self.moments(chain, total))

        def store_one(segment, values):
            start = GUARD + segment.start
            link.h1[:, start : start + segment.size, :] = values.astype(F32)

        self.narrow_norm(chain, link, NORM_Q1, link.n1, totals, link.n1, link.sl1, store_one)
        self.collect(chain, 2, link.h1, given.edges, link.t1)
        total = yield from self.scatter(link.z2, nt(link.t1[...], self.weight(TENSOR_S1)))
        link.n2[...] = total
        totals = yield from self.reduce(link.f2, self.moments(chain, total))
        self.narrow_norm(
            chain, link, NORM_S1, link.n2, totals, link.n2, link.sl2, into(link.h2.full)
        )
        yield from self.gather(link.h2)
        product = nn(self.joined(link.h2), self.weight(TENSOR_E1))
        link.n3[...] = product
        totals = yield from self.reduce(link.f3, self.moments(chain, product))
        for index, segment in enumerate(chain.segments):
            span = slice(segment.start, segment.stop)
            centre, factor = self.factors(
                totals[2 * index], totals[2 * index + 1], segment.count
            )
            link.facw[NORM_E1, index : index + 1, :] = factor
            normed = (link.n3[span, :] - centre) * factor
            link.n3[span, :] = normed
            joint = (normed * self.wide_row(NORM_E1, 0) + self.wide_row(NORM_E1, 1)) + (
                link.bypass[span, :] * self.wide_row(NORM_SC, 0) + self.wide_row(NORM_SC, 1)
            )
            logistic = jax.nn.sigmoid(joint)
            link.slq[span, :] = logistic * (1.0 + joint * (1.0 - logistic))
            widened = joint * logistic
            link.y[span, :] = widened
            link.r[span, :] = self.keep(segment, widened).astype(BF16)

        total = yield from self.scatter(link.u1, nt(link.r[...], self.weight(TENSOR_Q2)))
        link.n4[...] = total
        totals = yield from self.reduce(link.f4, self.moments(chain, total))

        def store_four(segment, values):
            start = GUARD + segment.start
            link.v1[start : start + segment.size, :] = values.astype(F32)

        self.narrow_norm(chain, link, NORM_Q2, link.n4, totals, link.n4, link.sl4, store_four)
        self.collect(chain, 1, link.v1, given.edges, link.t2)
        total = yield from self.scatter(link.u2, nt(link.t2[...], self.weight(TENSOR_S2)))
        link.n5[...] = total
        totals = yield from self.reduce(link.f5, self.moments(chain, total))
        self.narrow_norm(
            chain, link, NORM_S2, link.n5, totals, link.n5, link.sl5, into(link.v2.full)
        )
        yield from self.gather(link.v2)
        product = nn(self.joined(link.v2), self.weight(TENSOR_E2))
        link.n6[...] = product
        totals = yield from self.reduce(link.f6, self.moments(chain, product))

        terms = []
        for index, segment in enumerate(chain.segments):
            span = slice(segment.start, segment.stop)
            centre, factor = self.factors(
                totals[2 * index], totals[2 * index + 1], segment.count
            )
            link.facw[NORM_E2, index : index + 1, :] = factor
            normed = (link.n6[span, :] - centre) * factor
            link.n6[span, :] = normed
            gate = self.gates(link, span)
            final = link.y[span, :] + gate * (
                normed * self.wide_row(NORM_E2, 0) + self.wide_row(NORM_E2, 1)
            )
            logistic = jax.nn.sigmoid(final)
            made.out[span, :] = final * logistic
            slope = logistic * (1.0 + final * (1.0 - logistic))
            change = slope * given.cotangent[span, :].astype(F32)
            link.d2[span, :] = change
            gated = gate * change
            terms.append(self.sum_rows(gated))
            terms.append(self.sum_rows(gated * normed))
        totals = yield from self.reduce(link.r6, terms)
        gain_total = None
        offset_total = None
        for index, segment in enumerate(chain.segments):
            span = slice(segment.start, segment.stop)
            factor = link.facw[NORM_E2, index : index + 1, :]
            first, second = totals[2 * index], totals[2 * index + 1]
            gain_total = second if gain_total is None else gain_total + second
            offset_total = first if offset_total is None else offset_total + first
            change = (self.wide_row(NORM_E2, 0) * factor) * (
                self.gates(link, span) * link.d2[span, :]
                - first / segment.count
                - link.n6[span, :] * (second / segment.count)
            )
            link.du3[span, :] = self.keep(segment, change).astype(BF16)
        link.gw[4:5, :] = gain_total
        link.gw[5:6, :] = offset_total
        total = yield from self.scatter(link.b2, nt(link.du3[...], self.weight(TENSOR_E2)))
        gradients = total * link.sl5[...]
        link.d[0] = gradients
        totals = yield from self.reduce(link.r5, self.narrow_terms(chain, gradients, link.n5))
        self.narrow_back(
            chain, link, NORM_S2, link.d.at[0], totals, link.n5, into(link.g2.full)
        )
        yield from self.gather(link.g2)
        link.dt[GUARD : GUARD + rows, :] = nn(self.joined(link.g2), self.weight(TENSOR_S2))
        for segment, _, values in self.spread(chain, 1, link.dt, given.edges):
            span = slice(segment.start, segment.stop)
            link.d[0, span, :] = values * link.sl4[span, :]
        totals = yield from self.reduce(
            link.r4, self.narrow_terms(chain, link.d.at[0], link.n4)
        )
        self.narrow_back(
            chain, link, NORM_Q2, link.d.at[0], totals, link.n4, into(link.g1.full)
        )
        yield from self.gather(link.g1)

        link.d2[...] = (
            link.d2[...] + nn(self.joined(link.g1), self.weight(TENSOR_Q2))
        ) * link.slq[...]
        terms = []
        for segment in chain.segments:
            span = slice(segment.start, segment.stop)
            part = link.d2[span, :]
            terms.append(self.sum_rows(part))
            terms.append(self.sum_rows(part * link.n3[span, :]))
            terms.append(self.sum_rows(part * link.bypass[span, :]))
        totals = yield from self.reduce(link.r3, terms)
        sums = [None] * 3
        for index, segment in enumerate(chain.segments):
            span = slice(segment.start, segment.stop)
            part = link.d2[span, :]
            first = totals[3 * index]
            for which in range(3):
                value = totals[3 * index + which]
                sums[which] = value if sums[which] is None else sums[which] + value
            for norm, normed, target in (
                (NORM_E1, link.n3, link.dz3),
                (NORM_SC, link.bypass, link.dzp),
            ):
                factor = link.facw[norm, index : index + 1, :]
                second = totals[3 * index + 1 + norm]
                change = (self.wide_row(norm, 0) * factor) * (
                    part - first / segment.count - normed[span, :] * (second / segment.count)
                )
                target[span, :] = self.keep(segment, change).astype(BF16)
        link.gw[0:1, :] = sums[1]
        link.gw[1:2, :] = sums[0]
        link.gw[2:3, :] = sums[2]
        link.gw[3:4, :] = sums[0]
        total = yield from self.scatter(link.b1, nt(link.dz3[...], self.weight(TENSOR_E1)))
        gradients = total * link.sl2[...]
        link.d[0] = gradients
        totals = yield from self.reduce(link.r2, self.narrow_terms(chain, gradients, link.n2))
        self.narrow_back(
            chain, link, NORM_S1, link.d.at[0], totals, link.n2, into(link.k2.full)
        )
        yield from self.gather(link.k2)
        link.dt[GUARD : GUARD + rows, :] = nn(self.joined(link.k2), self.weight(TENSOR_S1))
        for segment, plane, values in self.spread(chain, 2, link.dt, given.edges):
            span = slice(segment.start, segment.stop)
            link.d[plane, span, :] = values * link.sl1[plane, span, :]
        totals = yield from self.reduce(link.r1, self.narrow_terms(chain, link.d, link.n1))

        def store_back_one(segment, values):
            for plane in range(4):
                start = plane * rows + segment.start
                link.k1.full[self.mp, start : start + segment.size, :] = values[plane]

        self.narrow_back(chain, link, NORM_Q1, link.d, totals, link.n1, store_back_one)
        yield from self.gather(link.k1)
        product = nn(self.joined(link.k1), self.weight(TENSOR_Q1))
        made.back[...] = product.reshape(4, rows, self.inner)

    def bypass_back(self, link):
        product = nt(link.dzp[...], self.weight(TENSOR_SC))
        total = yield from self.scatter(link.bx, product)
        link.back[...] = total


    def weight_product(self, tensor):
        total = None
        for link, given in zip(self.links, self.given.chains, strict=True):
            if tensor == TENSOR_Q1:
                pixels = given.pixels[...]
                part = tn(self.joined(link.k1), pixels.reshape(-1, self.inner))
            else:
                left, right = {
                    TENSOR_S1: (link.k2, link.t1),
                    TENSOR_E1: (link.h2, link.dz3),
                    TENSOR_SC: (link.xs, link.dzp),
                    TENSOR_Q2: (link.g1, link.r),
                    TENSOR_S2: (link.g2, link.t2),
                    TENSOR_E2: (link.v2, link.du3),
                }[tensor]
                part = tn(self.joined(left), right[...])
            total = part if total is None else total + part
        return total

    def weight_gradient(self, tensor):
        weight = self.weights[tensor]
        held = self.held[tensor]
        block, width, piece = weight.block, weight.width, weight.piece
        product = self.weight_product(tensor).astype(BF16)
        for tap in range(weight.taps):
            columns = product[:, tap * width : (tap + 1) * width]
            held.part[:, tap] = columns.reshape(self.mpn, block, width)
        theirs = self.half(block, 0, 1 - self.core)
        copy = self.remote(
            held.part.at[:, :, theirs, :],
            held.twin,
            held.twins.at[0],
            held.twins.at[1],
            (self.twin, self.mp),
        )
        copy.start()
        yield
        copy.wait()
        mine = held.part[:, :, self.half(block, 0, self.core), :]
        both = mine.astype(F32) + held.twin[...].astype(F32)
        for way in range(weight.ways):
            held.sums[way] = both[:, :, way * piece : (way + 1) * piece, :].astype(BF16)
        yield from (self.direct(held) if weight.direct else self.climb(held))
        copy = self.remote(
            held.fin, held.swap, held.swaps.at[0], held.swaps.at[1], (self.twin, self.mp)
        )
        copy.start()
        yield
        copy.wait()
        out = self.made.weights[tensor]
        copies = (
            pltpu.make_async_copy(held.fin, out.at[self.core], held.outs.at[0]),
            pltpu.make_async_copy(held.swap, out.at[1 - self.core], held.outs.at[1]),
        )
        for copy in copies:
            copy.start()
        yield
        for copy in copies:
            copy.wait()

    def mix(self, held, way, step, peer):
        return self.remote(
            held.sums.at[way, peer],
            held.fin.at[way, self.mp],
            held.mix_sent.at[step],
            held.mix_came.at[step],
            (self.dp, peer),
        )

    def mixed(self, held, way):
        for step, peer in enumerate(self.peers):
            self.mix(held, way, step, peer).wait_send()
            slot = held.fin.at[way, peer]
            self.remote(
                slot, slot, held.mix_sent.at[step], held.mix_came.at[step], (self.dp, peer)
            ).wait_recv()

    def direct(self, held):
        def above(level):
            return (level * 2 + self.core, self.mp)

        copies = []
        for step, level in enumerate(self.stack):
            copy = self.remote(
                held.sums.at[level],
                held.hop.at[self.z],
                held.hop_sent.at[step],
                held.hop_came.at[self.z],
                above(level),
            )
            copy.start()
            copies.append(copy)
        yield
        total = held.sums[self.z].astype(F32)
        for step, level in enumerate(self.stack):
            copies[step].wait_send()
            slot = held.hop.at[level]
            self.remote(
                slot, slot, held.hop_sent.at[step], held.hop_came.at[level], above(level)
            ).wait_recv()
            total = total + held.hop[level].astype(F32)
        held.sums[self.z] = total.astype(BF16)
        for step, peer in enumerate(self.peers):
            self.mix(held, self.z, step, peer).start()
        held.fin[self.z, self.mp] = held.sums[self.z, self.mp]
        yield
        self.mixed(held, self.z)
        mine = held.fin.at[self.z]
        copies = []
        for step, level in enumerate(self.stack):
            copy = self.remote(
                mine, mine, held.cast_sent.at[step], held.cast_came.at[self.z], above(level)
            )
            copy.start()
            copies.append(copy)
        yield
        for step, level in enumerate(self.stack):
            copies[step].wait_send()
            slot = held.fin.at[level]
            self.remote(
                slot, slot, held.cast_sent.at[step], held.cast_came.at[level], above(level)
            ).wait_recv()

    def climb(self, held):
        last = self.levels - 1

        def place(way, step):
            return step if way else last - step

        def onward(way):
            target = self.z + 1 if way else self.z - 1
            return (target * 2 + self.core, self.mp)

        def backward(way):
            target = self.z - 1 if way else self.z + 1
            return (target * 2 + self.core, self.mp)

        def hop(way, device):
            return self.remote(
                held.sums.at[way],
                held.hop.at[way],
                held.hop_sent.at[way],
                held.hop_came.at[way],
                device,
            )

        def cast(way, device):
            slot = held.fin.at[way]
            return self.remote(
                slot, slot, held.cast_sent.at[way], held.cast_came.at[way], device
            )

        for step in range(last + 1):
            for way in (0, 1):

                @pl.when(self.z == place(way, step))
                def _(way=way, step=step):
                    if step > 0:
                        hop(way, backward(way)).wait_recv()
                        total = held.sums[way].astype(F32) + held.hop[way].astype(F32)
                        held.sums[way] = total.astype(BF16)
                    if step < last:
                        hop(way, onward(way)).start()
                    else:
                        for index, peer in enumerate(self.peers):
                            self.mix(held, way, index, peer).start()
                        held.fin[way, self.mp] = held.sums[way, self.mp]

            yield
        for step in range(last, -1, -1):
            for way in (0, 1):

                @pl.when(self.z == place(way, step))
                def _(way=way, step=step):
                    if step == last:
                        self.mixed(held, way)
                    else:
                        hop(way, onward(way)).wait_send()
                        cast(way, onward(way)).wait_recv()
                    if step > 0:
                        cast(way, backward(way)).start()

            if step > 0:
                yield
        for way in (0, 1):

            @pl.when(self.z != place(way, 0))
            def _(way=way):
                cast(way, backward(way)).wait_send()


    def advance(self, tasks):
        for task in list(tasks):
            if next(task, self) is self:
                tasks.remove(task)

    def run(self):
        self.barrier()
        for tensor in (TENSOR_Q1, TENSOR_S1):
            self.weight_start(tensor)
        for chain, link in zip(self.chains, self.links, strict=True):
            self.clear(chain, link)
        parts = list(
            zip(self.chains, self.links, self.given.chains, self.made.chains, strict=True)
        )
        tasks = [self.chain(*part) for part in parts]
        background = []

        def start(tensor):
            return lambda: self.weight_start(tensor)

        def hand(tensor):
            return lambda: self.weight_pass(tensor)

        def grad(tensor):
            return lambda: background.append(self.weight_gradient(tensor))

        def bypass():
            for chain, link, given, _ in parts:
                background.append(self.bypass(chain, link, given.pixels))

        def bypass_back():
            for link in self.links:
                background.append(self.bypass_back(link))

        events = {
            1: (start(TENSOR_SC), bypass, start(TENSOR_E1)),
            2: (hand(TENSOR_S1), start(TENSOR_Q2)),
            4: (hand(TENSOR_SC), hand(TENSOR_E1), start(TENSOR_S2)),
            6: (hand(TENSOR_Q2), start(TENSOR_E2)),
            8: (hand(TENSOR_S2),),
            10: (hand(TENSOR_E2),),
            14: (grad(TENSOR_E2),),
            17: (grad(TENSOR_S2),),
            19: (grad(TENSOR_Q2),),
            20: (bypass_back, grad(TENSOR_E1), grad(TENSOR_SC)),
            23: (grad(TENSOR_S1),),
        }
        slot = 0
        while tasks:
            self.advance(tasks)
            slot += 1
            for event in events.get(slot, ()):
                event()
            self.advance(background)
        background.append(self.weight_gradient(TENSOR_Q1))
        self.advance(background)
        for link, made in zip(self.links, self.made.chains, strict=True):
            made.back[0] = made.back[0] + link.back[...]
        first, second = self.links
        self.made.mids[...] = first.gm[...] + second.gm[...]
        self.made.wides[...] = first.gw[...] + second.gw[...]
        while background:
            self.advance(background)


def kernel_text(trees, chains, weights, sizes, *refs):
    given_tree, made_tree, scratch_tree = trees
    given_size = given_tree.num_leaves
    made_size = made_tree.num_leaves
    given = jax.tree.unflatten(given_tree, refs[:given_size])
    made = jax.tree.unflatten(made_tree, refs[given_size : given_size + made_size])
    scratch = jax.tree.unflatten(scratch_tree, refs[given_size + made_size :])
    given = {**given, **dict(chains=[bag(value) for value in given["chains"]])}
    made = {**made, **dict(chains=[bag(value) for value in made["chains"]])}
    scratch = dict(
        chains=[bag(value) for value in scratch["chains"]],
        weights=[bag(value) for value in scratch["weights"]],
    )
    Body(bag(given), bag(made), bag(scratch), chains, weights, sizes).run()


def finish_text(chains, weights, sizes, *refs):
    mid, wide, inner, mpn = sizes
    count = len(weights)
    take = iter(refs)
    pieces = [next(take) for _ in range(count)]
    chain_in = [(next(take), next(take)) for _ in chains]
    mids, wides = next(take), next(take)
    outs = [next(take) for _ in range(count)]
    groups = [(next(take), next(take)) for _ in range(3)]
    mid_outs = [next(take) for _ in range(8)]
    wide_outs = [next(take) for _ in range(6)]
    near = [next(take) for _ in range(count)]
    wided = [next(take) for _ in range(count)]
    woven, came, gone, weave = next(take), next(take), next(take), next(take)
    arrivals = []
    for index in range(count):
        copy = pltpu.make_async_copy(pieces[index], near[index], came.at[index])
        copy.start()
        arrivals.append(copy)
    for row, out in enumerate(mid_outs):
        out[...] = mids[row, :]
    for row, out in enumerate(wide_outs):
        out[...] = wides[row, :]
    leaving = []
    for index, weight in enumerate(weights):
        arrivals[index].wait()
        width, piece = weight.width, weight.piece
        for core in range(2):
            for way in range(weight.ways):
                first = core * (weight.block // 2) + way * piece
                for source in range(mpn):
                    for tap in range(weight.taps):
                        wided[index][
                            tap, first : first + piece, source * width : (source + 1) * width
                        ] = near[index][core, way, source, tap].astype(F32)
        copy = pltpu.make_async_copy(wided[index], outs[index], gone.at[index])
        copy.start()
        leaving.append(copy)
    for chain, (out_rows, back_rows) in zip(chains, chain_in, strict=True):
        for segment in chain.segments:
            out, back = groups[segment.group]
            side = segment.side
            for i in range(side):
                if segment.inside:
                    for j in range(side):
                        start = segment.start + i * segment.down + j * segment.right
                        rows = slice(start, start + segment.images)
                        out[i, j] = out_rows[rows, :]
                        for plane in range(4):
                            back[2 * i + plane // 2, 2 * j + plane % 2] = back_rows[
                                plane, rows, :
                            ]
                    continue
                for image in range(segment.images):
                    start = segment.start + image * side * side + i * side
                    rows = slice(start, start + side)
                    out[image, i] = out_rows[rows, :]
                    for plane in range(4):
                        for lane in range(inner // LANE):
                            woven[
                                lane,
                                image,
                                2 * i + plane // 2,
                                pl.ds(plane % 2, side, stride=2),
                                :,
                            ] = back_rows[plane, rows, lane * LANE : (lane + 1) * LANE]
            if segment.inside:
                continue
            for lane in range(inner // LANE):
                copy = pltpu.make_async_copy(
                    woven.at[lane],
                    back.at[:, :, :, pl.ds(lane * LANE, LANE)],
                    weave.at[lane],
                )
                copy.start()
                leaving.append(copy)
    for copy in leaving:
        copy.wait()


def padded_rows(values, size):
    extra = size - values.shape[-2]
    if extra == 0:
        return values
    widths = [(0, 0)] * (values.ndim - 2) + [(0, extra), (0, 0)]
    return jnp.pad(values, widths)


def planes_of(segment, images):
    side = segment.side
    channels = images.shape[3]
    values = segment.pixel_first(images)
    if segment.inside:
        split = values.reshape(side, 2, side, 2, segment.images, channels)
        split = split.transpose(1, 3, 0, 2, 4, 5)
    else:
        split = values.reshape(segment.images, side, 2, side, 2, channels)
        split = split.transpose(2, 4, 0, 1, 3, 5)
    return padded_rows(split.reshape(4, segment.real, channels), segment.size)


def edge_masks(chain):
    masks = np.zeros((len(chain.segments), 4, chain.padded, LANE), np.float32)
    for place, segment in enumerate(chain.segments):
        index = np.arange(segment.real)
        down = index // segment.down % segment.side
        right = index // segment.right % segment.side
        start = GUARD + segment.start
        last = segment.side - 1
        for which, inside in enumerate((down > 0, down < last, right > 0, right < last)):
            masks[place, which, start : start + segment.real] = inside[:, None]
    return jnp.asarray(masks)


def fused_device(dpn, mpn, *args):
    images, widths, gates, cotangents = args[0:3], args[3], args[4:7], args[7:10]
    q1, s1, e1, sc, q2, s2, e2 = (args[index] for index in (10, 13, 16, 19, 22, 25, 28))
    mids = [args[index] for index in (11, 12, 14, 15, 23, 24, 26, 27)]
    wides = [args[index] for index in (17, 18, 20, 21, 29, 30)]
    mid = q1.shape[0]
    wide = wides[0].shape[0]
    inner = images[0].shape[3]
    shapes = [(values.shape[0], values.shape[1]) for values in images]
    chains = [Chain((2, 0), shapes, dpn), Chain((1,), shapes, dpn)]
    weights = weight_table(mid, wide, inner)
    sizes = (mid, wide, inner, dpn, mpn)
    vmem = pl.BlockSpec(memory_space=VMEM)
    smem = pl.BlockSpec(memory_space=pltpu.SMEM)
    anywhere = pl.BlockSpec(memory_space=pl.ANY)

    def by_tap(spatial):
        return spatial.transpose(1, 2, 0, 3).reshape(9, mid, mpn * mid)

    def rows_of(chain, build):
        return jnp.concatenate([build(s) for s in chain.segments], axis=-2)

    given = dict(
        chains=[
            dict(
                pixels=rows_of(chain, lambda s: planes_of(s, images[s.group])),
                cotangent=rows_of(
                    chain,
                    lambda s: padded_rows(
                        s.pixel_first(cotangents[s.group]).reshape(s.real, wide), s.size
                    ),
                ),
                edges=edge_masks(chain),
            )
            for chain in chains
        ],
        mids=mids,
        wides=wides,
        widths=widths,
        gates=list(gates),
        weights=[q1[None], by_tap(s1), e1[None], sc[None], q2[None], by_tap(s2), e2[None]],
    )
    given_specs = dict(
        chains=[dict(pixels=vmem, cotangent=vmem, edges=vmem) for _ in chains],
        mids=[vmem] * len(mids),
        wides=[vmem] * len(wides),
        widths=smem,
        gates=[smem] * 3,
        weights=[anywhere] * WEIGHTS,
    )
    shape = jax.ShapeDtypeStruct
    made = dict(
        chains=[
            dict(
                out=shape((chain.rows, wide), F32), back=shape((4, chain.rows, inner), F32)
            )
            for chain in chains
        ],
        mids=shape((8, mid), F32),
        wides=shape((8, wide), F32),
        weights=[
            shape((2, w.ways, mpn, w.taps, w.piece, w.width), BF16) for w in weights
        ],
    )
    made_specs = dict(
        chains=[dict(out=vmem, back=vmem) for _ in chains],
        mids=vmem,
        wides=vmem,
        weights=[anywhere] * WEIGHTS,
    )
    scratch = dict(
        chains=[chain_scratch(chain, mid, wide, inner, dpn, mpn) for chain in chains],
        weights=[weight_scratch(weight, dpn, mpn) for weight in weights],
    )
    trees = tuple(jax.tree.structure(tree) for tree in (given_specs, made_specs, scratch))
    results = pl.pallas_call(
        functools.partial(kernel_text, trees, chains, weights, sizes),
        out_shape=jax.tree.leaves(made),
        in_specs=jax.tree.leaves(given_specs),
        out_specs=jax.tree.leaves(made_specs),
        scratch_shapes=jax.tree.leaves(scratch),
        compiler_params=pltpu.CompilerParams(
            collective_id=0, has_side_effects=True, vmem_limit_bytes=62 * 2**20
        ),
        name="bottlenecks",
    )(*jax.tree.leaves(given))
    got = bag(jax.tree.unflatten(trees[1], results))

    final_shapes = [shape((w.taps, w.block, mpn * w.width), F32) for w in weights]
    segments = sorted((s for chain in chains for s in chain.segments), key=lambda s: s.group)

    def laid(s, side, channels):
        if s.inside:
            return shape((side, side, s.images, channels), F32)
        return shape((s.images, side, side, channels), F32)

    group_shapes = []
    for s in segments:
        group_shapes += [laid(s, s.side, wide), laid(s, 2 * s.side, inner)]
    woven = [laid(s, 2 * s.side, inner) for s in segments if not s.inside]
    vector_shapes = [shape((mid,), F32)] * 8 + [shape((wide,), F32)] * 6
    chain_in = []
    for value in got.chains:
        chain_in += [value["out"], value["back"]]
    final = pl.pallas_call(
        functools.partial(finish_text, chains, weights, (mid, wide, inner, mpn)),
        out_shape=final_shapes + group_shapes + vector_shapes,
        in_specs=[anywhere] * WEIGHTS + [vmem] * (len(chain_in) + 2),
        out_specs=[anywhere] * WEIGHTS
        + [spec for s in segments for spec in (vmem, vmem if s.inside else anywhere)]
        + [vmem] * len(vector_shapes),
        scratch_shapes=[VMEM(value.shape, BF16) for value in made["weights"]]
        + [VMEM(value.shape, F32) for value in final_shapes]
        + [VMEM((inner // LANE, *woven[0].shape[:3], LANE), F32)]
        + [DMA((WEIGHTS,)), DMA((WEIGHTS,)), DMA((inner // LANE,))],
        compiler_params=pltpu.CompilerParams(vmem_limit_bytes=48 * 2**20),
        name="finish",
    )(*got.weights, *chain_in, got.mids, got.wides)
    tensors = final[:WEIGHTS]
    grads = [value[0] for value in tensors]
    for place in (TENSOR_S1, TENSOR_S2):
        split = tensors[place].reshape(3, 3, mid, mpn * mid)
        grads[place] = split.transpose(2, 0, 1, 3)
    laid_out = final[WEIGHTS : WEIGHTS + 6]
    outputs = [s.image_first(laid_out[2 * s.group]) for s in segments]
    input_grads = [s.image_first(laid_out[2 * s.group + 1]) for s in segments]
    gm = final[WEIGHTS + 6 : WEIGHTS + 14]
    gw = final[WEIGHTS + 14 :]
    return (
        *outputs,
        *input_grads,
        grads[TENSOR_Q1],
        gm[0],
        gm[1],
        grads[TENSOR_S1],
        gm[2],
        gm[3],
        grads[TENSOR_E1],
        gw[0],
        gw[1],
        grads[TENSOR_SC],
        gw[2],
        gw[3],
        grads[TENSOR_Q2],
        gm[4],
        gm[5],
        grads[TENSOR_S2],
        gm[6],
        gm[7],
        grads[TENSOR_E2],
        gw[4],
        gw[5],
    )


def fits_kernel(mesh, args):
    mid = args[10].shape[0]
    inner = args[0].shape[3]
    wide = args[17].shape[0]
    return (
        mesh.shape["mp"] == 4
        and mesh.shape["dp"] == 8
        and mid == LANE
        and inner % LANE == 0
        and wide % LANE == 0
    )


def per_device(mesh, *args):
    if fits_kernel(mesh, args):
        return fused_device(mesh.shape["dp"], mesh.shape["mp"], *args)
    return on_device(*args)


def solution(mesh):
    in_specs = (
        P("dp", None, None, "mp"),
        P("dp", None, None, "mp"),
        P("dp", None, None, "mp"),
        P(),
        P("dp"),
        P("dp"),
        P("dp"),
        P("dp", None, None, "mp"),
        P("dp", None, None, "mp"),
        P("dp", None, None, "mp"),
        P("mp", None),
        P("mp"),
        P("mp"),
        P("mp", None, None, None),
        P("mp"),
        P("mp"),
        P("mp", None),
        P("mp"),
        P("mp"),
        P("mp", None),
        P("mp"),
        P("mp"),
        P("mp", None),
        P("mp"),
        P("mp"),
        P("mp", None, None, None),
        P("mp"),
        P("mp"),
        P("mp", None),
        P("mp"),
        P("mp"),
    )
    out_specs = (
        P("dp", None, None, "mp"),
        P("dp", None, None, "mp"),
        P("dp", None, None, "mp"),
        P("dp", None, None, "mp"),
        P("dp", None, None, "mp"),
        P("dp", None, None, "mp"),
        P("mp", None),
        P("mp"),
        P("mp"),
        P("mp", None, None, None),
        P("mp"),
        P("mp"),
        P("mp", None),
        P("mp"),
        P("mp"),
        P("mp", None),
        P("mp"),
        P("mp"),
        P("mp", None),
        P("mp"),
        P("mp"),
        P("mp", None, None, None),
        P("mp"),
        P("mp"),
        P("mp", None),
        P("mp"),
        P("mp"),
    )
    return jax.shard_map(
        functools.partial(per_device, mesh),
        mesh=mesh,
        in_specs=in_specs,
        out_specs=out_specs,
        check_vma=False,
    )
```

profile of v0, /device:TPU:0, one launch (start us, length us, event | category | flops | bytes accessed | tf_op | source)
XLA Modules:
  0.0 293.4 jit_solution(6770469766988326145)
XLA Ops:
  0.7 0.0 copy-start.13
  1.4 0.0 copy-start.12
  1.4 0.8 reshape_transpose.6
  2.2 0.9 reshape_transpose.7
  3.3 1.0 reshape.87
  4.2 0.7 fusion.5.refs_0_
  5.0 0.0 copy-done.13
  5.0 0.1 reshape.91
  5.0 0.7 pad.28.refs_3_
  5.7 0.0 copy-done.12
  5.7 0.1 copy.72
  5.9 0.1 reshape.89
  6.0 0.8 fusion.2.refs_2_
  6.8 0.0 copy-done.11
  6.8 0.3 reshape.92
  7.1 0.3 copy.71
  7.5 0.2 reshape.93
  7.7 0.1 copy.67
  7.8 0.8 pad.29.refs_5_
  8.6 266.2 %bottlenecks.1 = (f32[4,240,256]{2,1,0:T(8,128)}, f32[240,512]{1,0:T(8,128)}, f32[4,224,256]{2,1,0:T(8,128)}, f32[224,512]{1,0:T(8,128)}, f32[8,128]{1,0:T(8,128...) custom-call(bf16[240,512]{1,0:T(8,128)(2,1)} %fusion.5.refs_0_, ...), custom_call_target="tpu_custom_call" | custom-call | tf_op jit(solution)/shard_map/bottlenecks/pallas_call | solution.py:1776
  274.8 1.2 copy-done
  276.0 1.2 copy-done.1
  277.2 1.2 copy-done.2
  278.4 1.0 copy-done.3
  279.5 1.0 copy-done.4
  280.5 1.0 copy-done.5
  281.6 1.0 copy-done.6
  282.6 1.0 copy-done.7
  283.6 0.9 copy-done.8
  284.6 0.7 copy-done.9
  285.3 0.7 copy-done.10
  285.9 7.2 %finish.1 = (f32[1,128,1024]{2,1,0:T(8,128)}, f32[9,128,512]{2,1,0:T(8,128)}, f32[1,128,2048]{2,1,0:T(8,128)}, f32[1,256,2048]{2,1,0:T(8,128)}, f32[1,128,2048]{...) custom-call(bf16[2,4,4,1,16,256]{5,4,3,2,1,0:T(8,128)(2,1)S(1)} %cop, ...), custom_call_target="tpu_custom_call" | custom-call | tf_op jit(solution)/shard_map/finish/pallas_call | solution.py:1805
  (15 shorter events, 0.1 us)
Async XLA Ops:
  0.7 4.3 %copy-start.13 = (bf16[6,6,6,512]{3,2,1,0:T(8,128)(2,1)S(1)}, bf16[6,6,6,512]{3,2,1,0:T(8,128)(2,1)}, u32[]{:S(2)}) copy-start(bf16[6,6,6,512]{3,2,1,0:T(8,128)(2,1)} %param.41) | copy-start | bytes 663556
  1.4 4.4 %copy-start.12 = (bf16[4,14,14,256]{3,0,2,1:T(4,128)(2,1)S(1)}, bf16[4,14,14,256]{3,0,2,1:T(4,128)(2,1)}, u32[]{:S(2)}) copy-start(bf16[4,14,14,256]{3,0,2,1:T(4,128)(2,1)} %param.35) | copy-start | bytes 1204228
  5.7 1.1 copy-start.11
  274.8 1.2 copy-start
  276.0 1.2 copy-start.1
  277.2 1.2 copy-start.2
  278.4 1.0 copy-start.3
  279.5 1.0 copy-start.4
  280.5 1.0 copy-start.5
  281.5 1.0 copy-start.6
  282.6 1.0 copy-start.7
  283.6 0.9 copy-start.8
  284.5 0.7 copy-start.9
  285.3 0.7 copy-start.10
where the time goes:
time: 294 us; the launch traced here: 293 us
  Pallas kernels  273 us (93%)
  local copies, waits for them, and re-layouts  16.7 us (6%)
    pallas_call x1, Pallas kernels, fused_device(): pl.pallas_call(functools.partial(kernel_text, trees, chains, weights, siz...  266 us
    unnamed x28, local copies, waits for them, and re-layouts  11.1 us
    pallas_call x1, Pallas kernels, fused_device(): pl.pallas_call(functools.partial(finish_text, chains, weights, (mid, wide...  7.24 us

commit v1 on v0

--- a/solution.py
+++ b/solution.py
@@ -594,25 +594,55 @@
 
 
 class Weight:
-    def __init__(self, block, width, taps, direct):
+    def __init__(self, block, width, taps):
         self.block = block
         self.width = width
         self.taps = taps
+
+
+def weight_table(mid, wide, inner):
+    return [
+        Weight(mid, inner, 1),
+        Weight(mid, mid, 9),
+        Weight(mid, wide, 1),
+        Weight(inner, wide, 1),
+        Weight(mid, wide, 1),
+        Weight(mid, mid, 9),
+        Weight(mid, wide, 1),
+    ]
+
+
+class Unit:
+    def __init__(self, tensor, weight, part, parts, direct=False):
+        self.tensor = tensor
+        self.block = weight.block
+        self.taps = weight.taps // parts if weight.taps > 1 else 1
+        self.width = weight.width if weight.taps > 1 else weight.width // parts
+        self.first_tap = part * self.taps if weight.taps > 1 else 0
+        self.first_column = 0 if weight.taps > 1 else part * self.width
+        self.span = self.taps * self.width
+        self.columns = slice(part * self.span, (part + 1) * self.span)
         self.direct = direct
         self.ways = 4 if direct else 2
-        self.piece = block // (2 * self.ways)
-
-
-def weight_table(mid, wide, inner):
-    return [
-        Weight(mid, inner, 1, True),
-        Weight(mid, mid, 9, True),
-        Weight(mid, wide, 1, False),
-        Weight(inner, wide, 1, True),
-        Weight(mid, wide, 1, False),
-        Weight(mid, mid, 9, True),
-        Weight(mid, wide, 1, False),
-    ]
+        self.piece = weight.block // (2 * self.ways)
+
+
+def unit_table(weights):
+    units = []
+    for tensor, parts in (
+        (TENSOR_E2, 1),
+        (TENSOR_S2, 3),
+        (TENSOR_Q2, 1),
+        (TENSOR_E1, 1),
+        (TENSOR_SC, 2),
+        (TENSOR_S1, 3),
+        (TENSOR_Q1, 1),
+    ):
+        for part in range(parts):
+            units.append(
+                Unit(tensor, weights[tensor], part, parts, direct=tensor == TENSOR_Q1)
+            )
+    return units
 
 
 def chain_scratch(chain, mid, wide, inner, dpn, mpn):
@@ -624,18 +654,15 @@
         return dict(
             send=VMEM((mpn, lead, width), BF16),
             recv=VMEM((near, lead, width), BF16),
-            sent=DMA((near,)),
-            came=DMA((near,)),
+            sems=DMA((2,)),
         )
 
     def gathered(lead, width):
-        return dict(full=VMEM((mpn, lead, width), BF16), sent=DMA((near,)), came=DMA((near,)))
+        return dict(full=VMEM((mpn, lead, width), BF16), sems=DMA((2,)))
 
     def reduced(terms, width):
         depth = -(-(len(chain.segments) * terms * width // LANE) // 8) * 8
-        return dict(
-            stat=VMEM((dpn, depth, LANE), F32), sent=DMA((dpn - 1,)), came=DMA((dpn,))
-        )
+        return dict(stat=VMEM((dpn, depth, LANE), F32), sems=DMA((2,)))
 
     return dict(
         z1=summed(4 * rows, mid),
@@ -698,18 +725,21 @@
     )
 
 
-def weight_scratch(weight, dpn, mpn):
-    near = mpn - 1
-    spread = (mpn, weight.taps, weight.block // 2, weight.width)
-    pieces = (weight.ways, mpn, weight.taps, weight.piece, weight.width)
+def weight_scratch(weight, mpn):
     return dict(
         full=VMEM((weight.taps, mpn * weight.block, weight.width), BF16),
-        sent=DMA((near,)),
-        came=DMA((near,)),
-        passed=DMA((near,)),
-        given=DMA((near,)),
+        fetch=DMA((2,)),
+        lift=DMA((2,)),
+        hand=DMA((2,)),
         own=DMA((1,)),
-        part=VMEM((mpn, weight.taps, weight.block, weight.width), BF16),
+    )
+
+
+def unit_scratch(unit, mpn):
+    spread = (mpn, unit.taps, unit.block // 2, unit.width)
+    pieces = (unit.ways, mpn, unit.taps, unit.piece, unit.width)
+    return dict(
+        part=VMEM((mpn, unit.taps, unit.block, unit.width), BF16),
         twin=VMEM(spread, BF16),
         sums=VMEM(pieces, BF16),
         hop=VMEM(pieces, BF16),
@@ -718,22 +748,25 @@
         twins=DMA((2,)),
         swaps=DMA((2,)),
         outs=DMA((2,)),
-        hop_sent=DMA((4,)),
-        hop_came=DMA((4,)),
-        mix_sent=DMA((near,)),
-        mix_came=DMA((near,)),
-        cast_sent=DMA((4,)),
-        cast_came=DMA((4,)),
+        hop_sent=DMA((2,)),
+        hop_came=DMA((2,)),
+        mix=DMA((2,)),
+        cast_sent=DMA((2,)),
+        cast_came=DMA((2,)),
     )
 
 
 class Body:
-    def __init__(self, given, made, scratch, chains, weights, sizes):
+    def __init__(self, given, made, scratch, chains, weights, units, sizes):
         self.given = given
         self.made = made
         self.links = scratch.chains
         self.weights = weights
         self.held = scratch.weights
+        self.units = units
+        self.places = classes(units)[2]
+        self.rows = Rows(chains, sizes[1], sizes[2])
+        self.sums = scratch.units
         self.chains = chains
         self.mid, self.wide, self.inner, self.dpn, self.mpn = sizes
         self.dp = lax.axis_index("dp")
@@ -752,8 +785,11 @@
         self.others = [lax.rem(self.dp + step, self.dpn) for step in range(1, self.dpn)]
         self.stack = [lax.rem(self.z + step, self.levels) for step in range(1, self.levels)]
         self.flying = {}
-        self.passing = {}
+        self.fetched = set()
+        self.lifting = {}
+        self.passing = set()
         self.present = set()
+        self.background = []
 
     def barrier(self):
         semaphore = pltpu.get_barrier_semaphore()
@@ -778,52 +814,39 @@
         )
 
 
+    def settle(self, slab, sems, device):
+        copy = self.remote(slab, slab, sems.at[0], sems.at[1], device)
+        copy.wait_send()
+        copy.wait_recv()
+
     def scatter(self, link, values):
         width = link.send.shape[2]
         for block in range(self.mpn):
             link.send[block] = values[:, block * width : (block + 1) * width].astype(BF16)
-        copies = []
         for step, peer in enumerate(self.peers):
-            copy = self.remote(
+            self.remote(
                 link.send.at[peer],
                 link.recv.at[step],
-                link.sent.at[step],
-                link.came.at[step],
+                link.sems.at[0],
+                link.sems.at[1],
                 (self.dp, peer),
-            )
-            copy.start()
-            copies.append(copy)
+            ).start()
         yield
-        for copy in copies:
-            copy.wait()
+        self.settle(link.recv, link.sems, (self.dp, self.peers[0]))
         total = link.send[self.mp].astype(F32)
         for step in range(self.mpn - 1):
             total = total + link.recv[step].astype(F32)
         return total
 
     def gather(self, link):
-        full = link.full
-        copies = []
-        for step, peer in enumerate(self.peers):
-            copy = self.remote(
-                full.at[self.mp],
-                full.at[self.mp],
-                link.sent.at[step],
-                link.came.at[step],
-                (self.dp, peer),
-            )
-            copy.start()
-            copies.append(copy)
+        mine = link.full.at[self.mp]
+        for peer in self.peers:
+            self.remote(
+                mine, mine, link.sems.at[0], link.sems.at[1], (self.dp, peer)
+            ).start()
         yield
-        for step, peer in enumerate(self.peers):
-            copies[step].wait_send()
-            self.remote(
-                full.at[peer],
-                full.at[peer],
-                link.sent.at[step],
-                link.came.at[step],
-                (self.dp, peer),
-            ).wait_recv()
+        slab = link.full.at[pl.ds(0, self.mpn - 1)]
+        self.settle(slab, link.sems, (self.dp, self.peers[0]))
 
     def joined(self, link):
         return jnp.concatenate([link.full[block] for block in range(self.mpn)], axis=1)
@@ -838,27 +861,14 @@
         if depth > len(lines):
             lines.append(jnp.zeros((depth - len(lines), LANE), F32))
         stat[self.dp] = jnp.concatenate(lines, axis=0)
-        copies = []
-        for step, other in enumerate(self.others):
-            copy = self.remote(
-                stat.at[self.dp],
-                stat.at[self.dp],
-                link.sent.at[step],
-                link.came.at[self.dp],
-                (other, self.mp),
-            )
-            copy.start()
-            copies.append(copy)
+        mine = stat.at[self.dp]
+        for other in self.others:
+            self.remote(
+                mine, mine, link.sems.at[0], link.sems.at[1], (other, self.mp)
+            ).start()
         yield
-        for step, other in enumerate(self.others):
-            copies[step].wait_send()
-            self.remote(
-                stat.at[other],
-                stat.at[other],
-                link.sent.at[step],
-                link.came.at[other],
-                (other, self.mp),
-            ).wait_recv()
+        slab = stat.at[pl.ds(0, self.dpn - 1)]
+        self.settle(slab, link.sems, (self.others[0], self.mp))
         total = stat[0]
         for source in range(1, self.dpn):
             total = total + stat[source]
@@ -873,6 +883,19 @@
     def half(self, block, first, core):
         return pl.ds(pl.multiple_of(first + core * (block // 2), 16), block // 2)
 
+    def eighth(self, block, first, core, level):
+        size = block // (2 * self.levels)
+        return pl.ds(pl.multiple_of(first + core * (block // 2) + level * size, 16), size)
+
+    def shared(self, tensor):
+        return tensor != TENSOR_Q1
+
+    def mine(self, tensor, first):
+        block = self.weights[tensor].block
+        if self.shared(tensor):
+            return self.eighth(block, first, self.core, self.z)
+        return self.half(block, first, self.core)
+
     def weight_start(self, tensor):
         weight = self.weights[tensor]
         held = self.held[tensor]
@@ -882,58 +905,79 @@
         def columns(device):
             return pl.ds(pl.multiple_of(device * width, LANE), width)
 
-        copies = []
-        for step, peer in enumerate(self.peers):
-            copy = self.remote(
-                source.at[:, self.half(block, 0, self.core), columns(peer)],
-                held.full.at[:, self.half(block, self.mp * block, self.core), :],
-                held.sent.at[step],
-                held.came.at[step],
+        for peer in self.peers:
+            self.remote(
+                source.at[:, self.mine(tensor, 0), columns(peer)],
+                held.full.at[:, self.mine(tensor, self.mp * block), :],
+                held.fetch.at[0],
+                held.fetch.at[1],
                 (self.dp, peer),
-            )
-            copy.start()
-            copies.append(copy)
+            ).start()
         own = pltpu.make_async_copy(
             source.at[:, :, columns(self.mp)],
             held.full.at[:, pl.ds(pl.multiple_of(self.mp * block, 16), block), :],
             held.own.at[0],
         )
         own.start()
-        self.flying[tensor] = (copies, own)
+        self.flying[tensor] = own
+
+    def slab(self, tensor, rows):
+        return self.held[tensor].full.at[:, pl.ds(0, rows), :]
+
+    def weight_fetched(self, tensor):
+        if tensor in self.fetched:
+            return
+        block = self.weights[tensor].block
+        rows = block // (2 * self.levels) if self.shared(tensor) else block // 2
+        held = self.held[tensor]
+        slab = self.slab(tensor, len(self.peers) * rows)
+        self.settle(slab, held.fetch, (self.dp, self.peers[0]))
+        self.flying[tensor].wait()
+        self.fetched.add(tensor)
+
+    def weight_lift(self, tensor, steps=(0, 1, 2)):
+        self.weight_fetched(tensor)
+        block = self.weights[tensor].block
+        held = self.held[tensor]
+        for step in steps:
+            came = held.full.at[:, self.mine(tensor, self.peers[step] * block), :]
+            for level in self.stack:
+                self.remote(
+                    came,
+                    came,
+                    held.lift.at[0],
+                    held.lift.at[1],
+                    (level * 2 + self.core, self.mp),
+                ).start()
+        self.lifting[tensor] = self.lifting.get(tensor, ()) + tuple(steps)
 
     def weight_pass(self, tensor):
         if tensor in self.passing:
             return
-        copies, own = self.flying[tensor]
+        self.passing.add(tensor)
+        self.weight_fetched(tensor)
         block = self.weights[tensor].block
         held = self.held[tensor]
-        passed = []
-        for step, peer in enumerate(self.peers):
+        if self.shared(tensor):
+            rest = [step for step in range(3) if step not in self.lifting.get(tensor, ())]
+            if rest:
+                self.weight_lift(tensor, rest)
+            rows = block // (2 * self.levels) * len(self.peers) * len(self.stack)
+            slab = self.slab(tensor, rows)
+            self.settle(slab, held.lift, (self.stack[0] * 2 + self.core, self.mp))
+        for peer in self.peers:
             came = held.full.at[:, self.half(block, peer * block, self.core), :]
-            copies[step].wait_send()
             self.remote(
-                came, came, held.sent.at[step], held.came.at[step], (self.dp, peer)
-            ).wait_recv()
-            copy = self.remote(
-                came, came, held.passed.at[step], held.given.at[step], (self.twin, self.mp)
-            )
-            copy.start()
-            passed.append(copy)
-        own.wait()
-        self.passing[tensor] = passed
+                came, came, held.hand.at[0], held.hand.at[1], (self.twin, self.mp)
+            ).start()
 
     def weight(self, tensor):
         held = self.held[tensor]
         weight = self.weights[tensor]
-        block = weight.block
         if tensor not in self.present:
             self.weight_pass(tensor)
-            for step, peer in enumerate(self.peers):
-                rest = held.full.at[:, self.half(block, peer * block, 1 - self.core), :]
-                self.passing[tensor][step].wait_send()
-                self.remote(
-                    rest, rest, held.passed.at[step], held.given.at[step], (self.twin, self.mp)
-                ).wait_recv()
+            slab = self.slab(tensor, len(self.peers) * (weight.block // 2))
+            self.settle(slab, held.hand, (self.twin, self.mp))
             self.present.add(tensor)
         if weight.taps == 1:
             return held.full[0]
@@ -1121,8 +1165,9 @@
             link.facw[NORM_SC, index : index + 1, :] = factor
             link.bypass[rows, :] = (link.bypass[rows, :] - centre) * factor
 
-    def chain(self, chain, link, given, made):
+    def chain(self, chain, link, given, place):
         rows = chain.rows
+        start = self.rows.start[place]
         mid = self.mid
 
         def into(full):
@@ -1205,7 +1250,7 @@
                 normed * self.wide_row(NORM_E2, 0) + self.wide_row(NORM_E2, 1)
             )
             logistic = jax.nn.sigmoid(final)
-            made.out[span, :] = final * logistic
+            self.made.rows[start + segment.start : start + segment.stop, :] = final * logistic
             slope = logistic * (1.0 + final * (1.0 - logistic))
             change = slope * given.cotangent[span, :].astype(F32)
             link.d2[span, :] = change
@@ -1304,7 +1349,12 @@
         self.narrow_back(chain, link, NORM_Q1, link.d, totals, link.n1, store_back_one)
         yield from self.gather(link.k1)
         product = nn(self.joined(link.k1), self.weight(TENSOR_Q1))
-        made.back[...] = product.reshape(4, rows, self.inner)
+        for plane in range(4):
+            first, columns = self.rows.plane(place, plane)
+            values = product[plane * rows : (plane + 1) * rows, :]
+            if plane == 0:
+                values = values + link.back[...]
+            self.made.rows[first : first + rows, columns] = values
 
     def bypass_back(self, link):
         product = nt(link.dzp[...], self.weight(TENSOR_SC))
@@ -1312,10 +1362,10 @@
         link.back[...] = total
 
 
-    def weight_product(self, tensor):
+    def unit_product(self, unit):
         total = None
         for link, given in zip(self.links, self.given.chains, strict=True):
-            if tensor == TENSOR_Q1:
+            if unit.tensor == TENSOR_Q1:
                 pixels = given.pixels[...]
                 part = tn(self.joined(link.k1), pixels.reshape(-1, self.inner))
             else:
@@ -1326,17 +1376,17 @@
                     TENSOR_Q2: (link.g1, link.r),
                     TENSOR_S2: (link.g2, link.t2),
                     TENSOR_E2: (link.v2, link.du3),
-                }[tensor]
-                part = tn(self.joined(left), right[...])
+                }[unit.tensor]
+                part = tn(self.joined(left), right[:, unit.columns])
             total = part if total is None else total + part
         return total
 
-    def weight_gradient(self, tensor):
-        weight = self.weights[tensor]
-        held = self.held[tensor]
-        block, width, piece = weight.block, weight.width, weight.piece
-        product = self.weight_product(tensor).astype(BF16)
-        for tap in range(weight.taps):
+    def unit_gradient(self, index):
+        unit = self.units[index]
+        held = self.sums[index]
+        block, width, piece = unit.block, unit.width, unit.piece
+        product = self.unit_product(unit).astype(BF16)
+        for tap in range(unit.taps):
             columns = product[:, tap * width : (tap + 1) * width]
             held.part[:, tap] = columns.reshape(self.mpn, block, width)
         theirs = self.half(block, 0, 1 - self.core)
@@ -1348,92 +1398,82 @@
             (self.twin, self.mp),
         )
         copy.start()
-        yield
+        yield 1
         copy.wait()
         mine = held.part[:, :, self.half(block, 0, self.core), :]
         both = mine.astype(F32) + held.twin[...].astype(F32)
-        for way in range(weight.ways):
+        for way in range(unit.ways):
             held.sums[way] = both[:, :, way * piece : (way + 1) * piece, :].astype(BF16)
-        yield from (self.direct(held) if weight.direct else self.climb(held))
+        yield from (self.direct(held) if unit.direct else self.climb(held))
         copy = self.remote(
             held.fin, held.swap, held.swaps.at[0], held.swaps.at[1], (self.twin, self.mp)
         )
         copy.start()
-        yield
+        yield 1
         copy.wait()
-        out = self.made.weights[tensor]
+        which, place = self.places[index]
+        out = self.made.units[which].at[place]
         copies = (
             pltpu.make_async_copy(held.fin, out.at[self.core], held.outs.at[0]),
             pltpu.make_async_copy(held.swap, out.at[1 - self.core], held.outs.at[1]),
         )
         for copy in copies:
             copy.start()
-        yield
+        yield 1
         for copy in copies:
             copy.wait()
 
-    def mix(self, held, way, step, peer):
-        return self.remote(
-            held.sums.at[way, peer],
-            held.fin.at[way, self.mp],
-            held.mix_sent.at[step],
-            held.mix_came.at[step],
-            (self.dp, peer),
-        )
+    def mix(self, held, way):
+        for peer in self.peers:
+            self.remote(
+                held.sums.at[way, peer],
+                held.fin.at[way, self.mp],
+                held.mix.at[0],
+                held.mix.at[1],
+                (self.dp, peer),
+            ).start()
+        held.fin[way, self.mp] = held.sums[way, self.mp]
 
     def mixed(self, held, way):
-        for step, peer in enumerate(self.peers):
-            self.mix(held, way, step, peer).wait_send()
-            slot = held.fin.at[way, peer]
-            self.remote(
-                slot, slot, held.mix_sent.at[step], held.mix_came.at[step], (self.dp, peer)
-            ).wait_recv()
+        slab = held.fin.at[way, pl.ds(0, len(self.peers))]
+        self.settle(slab, held.mix, (self.dp, self.peers[0]))
 
     def direct(self, held):
         def above(level):
             return (level * 2 + self.core, self.mp)
 
-        copies = []
-        for step, level in enumerate(self.stack):
-            copy = self.remote(
+        first = above(self.stack[0])
+        others = pl.ds(0, len(self.stack))
+        for level in self.stack:
+            self.remote(
                 held.sums.at[level],
                 held.hop.at[self.z],
-                held.hop_sent.at[step],
-                held.hop_came.at[self.z],
+                held.hop_sent.at[0],
+                held.hop_came.at[0],
                 above(level),
-            )
-            copy.start()
-            copies.append(copy)
-        yield
+            ).start()
+        yield 2
+        slab = held.hop.at[others]
+        copy = self.remote(slab, slab, held.hop_sent.at[0], held.hop_came.at[0], first)
+        copy.wait_send()
+        copy.wait_recv()
         total = held.sums[self.z].astype(F32)
-        for step, level in enumerate(self.stack):
-            copies[step].wait_send()
-            slot = held.hop.at[level]
-            self.remote(
-                slot, slot, held.hop_sent.at[step], held.hop_came.at[level], above(level)
-            ).wait_recv()
+        for level in self.stack:
             total = total + held.hop[level].astype(F32)
         held.sums[self.z] = total.astype(BF16)
-        for step, peer in enumerate(self.peers):
-            self.mix(held, self.z, step, peer).start()
-        held.fin[self.z, self.mp] = held.sums[self.z, self.mp]
-        yield
+        self.mix(held, self.z)
+        yield 2
         self.mixed(held, self.z)
         mine = held.fin.at[self.z]
-        copies = []
-        for step, level in enumerate(self.stack):
-            copy = self.remote(
-                mine, mine, held.cast_sent.at[step], held.cast_came.at[self.z], above(level)
-            )
-            copy.start()
-            copies.append(copy)
-        yield
-        for step, level in enumerate(self.stack):
-            copies[step].wait_send()
-            slot = held.fin.at[level]
+        for level in self.stack:
             self.remote(
-                slot, slot, held.cast_sent.at[step], held.cast_came.at[level], above(level)
-            ).wait_recv()
+                mine, mine, held.cast_sent.at[0], held.cast_came.at[0], above(level)
+            ).start()
+        yield 2
+        slab = held.fin.at[others]
+        copy = self.remote(slab, slab, held.cast_sent.at[0], held.cast_came.at[0], first)
+        copy.wait_send()
+        copy.wait_recv()
 
     def climb(self, held):
         last = self.levels - 1
@@ -1476,11 +1516,9 @@
                     if step < last:
                         hop(way, onward(way)).start()
                     else:
-                        for index, peer in enumerate(self.peers):
-                            self.mix(held, way, index, peer).start()
-                        held.fin[way, self.mp] = held.sums[way, self.mp]
-
-            yield
+                        self.mix(held, way)
+
+            yield 2
         for step in range(last, -1, -1):
             for way in (0, 1):
 
@@ -1495,7 +1533,7 @@
                         cast(way, backward(way)).start()
 
             if step > 0:
-                yield
+                yield 2
         for way in (0, 1):
 
             @pl.when(self.z != place(way, 0))
@@ -1503,72 +1541,135 @@
                 cast(way, backward(way)).wait_send()
 
 
-    def advance(self, tasks):
-        for task in list(tasks):
-            if next(task, self) is self:
-                tasks.remove(task)
+    def launch(self, task):
+        self.background.append([task, 0])
+
+    def advance(self):
+        for entry in list(self.background):
+            entry[1] -= 1
+            if entry[1] > 0:
+                continue
+            pause = next(entry[0], self)
+            if pause is self:
+                self.background.remove(entry)
+            else:
+                entry[1] = pause or 1
 
     def run(self):
         self.barrier()
-        for tensor in (TENSOR_Q1, TENSOR_S1):
+        for tensor in (TENSOR_Q1, TENSOR_S1, TENSOR_E1, TENSOR_SC, TENSOR_Q2):
             self.weight_start(tensor)
         for chain, link in zip(self.chains, self.links, strict=True):
             self.clear(chain, link)
-        parts = list(
-            zip(self.chains, self.links, self.given.chains, self.made.chains, strict=True)
-        )
+        parts = [
+            (chain, link, given, place)
+            for place, (chain, link, given) in enumerate(
+                zip(self.chains, self.links, self.given.chains, strict=True)
+            )
+        ]
         tasks = [self.chain(*part) for part in parts]
-        background = []
 
         def start(tensor):
             return lambda: self.weight_start(tensor)
 
+        def lift(tensor, steps=(0, 1, 2)):
+            return lambda: self.weight_lift(tensor, steps)
+
         def hand(tensor):
             return lambda: self.weight_pass(tensor)
 
-        def grad(tensor):
-            return lambda: background.append(self.weight_gradient(tensor))
-
-        def bypass():
-            for chain, link, given, _ in parts:
-                background.append(self.bypass(chain, link, given.pixels))
-
-        def bypass_back():
-            for link in self.links:
-                background.append(self.bypass_back(link))
+        def grad(tensor, part=0):
+            places = [place for place, unit in enumerate(self.units) if unit.tensor == tensor]
+            return lambda: self.launch(self.unit_gradient(places[part]))
+
+        def bypass(index):
+            chain, link, given, _ = parts[index]
+            return lambda: self.launch(self.bypass(chain, link, given.pixels))
+
+        def bypass_back(index):
+            return lambda: self.launch(self.bypass_back(self.links[index]))
 
         events = {
-            1: (start(TENSOR_SC), bypass, start(TENSOR_E1)),
-            2: (hand(TENSOR_S1), start(TENSOR_Q2)),
-            4: (hand(TENSOR_SC), hand(TENSOR_E1), start(TENSOR_S2)),
-            6: (hand(TENSOR_Q2), start(TENSOR_E2)),
+            1: (lift(TENSOR_S1), lift(TENSOR_E1), lift(TENSOR_SC), lift(TENSOR_Q2)),
+            2: (bypass(0), start(TENSOR_S2), start(TENSOR_E2), hand(TENSOR_S1)),
+            3: (lift(TENSOR_S2, (0, 1)),),
+            4: (bypass(1), hand(TENSOR_E1), hand(TENSOR_SC)),
+            5: (lift(TENSOR_S2, (2,)),),
+            6: (hand(TENSOR_Q2),),
+            7: (lift(TENSOR_E2),),
             8: (hand(TENSOR_S2),),
             10: (hand(TENSOR_E2),),
             14: (grad(TENSOR_E2),),
-            17: (grad(TENSOR_S2),),
-            19: (grad(TENSOR_Q2),),
-            20: (bypass_back, grad(TENSOR_E1), grad(TENSOR_SC)),
-            23: (grad(TENSOR_S1),),
+            17: (grad(TENSOR_S2, 0),),
+            18: (grad(TENSOR_S2, 1),),
+            19: (grad(TENSOR_S2, 2), grad(TENSOR_Q2)),
+            20: (grad(TENSOR_E1),),
+            21: (bypass_back(0), grad(TENSOR_SC, 0)),
+            22: (grad(TENSOR_SC, 1),),
+            23: (
+                bypass_back(1),
+                grad(TENSOR_S1, 0),
+                grad(TENSOR_S1, 1),
+                grad(TENSOR_S1, 2),
+            ),
         }
         slot = 0
         while tasks:
-            self.advance(tasks)
             slot += 1
+            for place, task in enumerate(list(tasks)):
+                if next(task, self) is self:
+                    tasks.remove(task)
+                if place == 0:
+                    self.advance()
             for event in events.get(slot, ()):
                 event()
-            self.advance(background)
-        background.append(self.weight_gradient(TENSOR_Q1))
-        self.advance(background)
-        for link, made in zip(self.links, self.made.chains, strict=True):
-            made.back[0] = made.back[0] + link.back[...]
+            self.advance()
+            if slot == 24:
+                for _ in range(8):
+                    self.advance()
+        self.launch(self.unit_gradient(len(self.units) - 1))
+        self.advance()
         first, second = self.links
-        self.made.mids[...] = first.gm[...] + second.gm[...]
-        self.made.wides[...] = first.gw[...] + second.gw[...]
-        while background:
-            self.advance(background)
-
-
-def kernel_text(trees, chains, weights, sizes, *refs):
+        mids, wides = self.rows.mids, self.rows.wides
+        self.made.rows[mids : mids + 8, : self.mid] = first.gm[...] + second.gm[...]
+        self.made.rows[wides : wides + 8, :] = first.gw[...] + second.gw[...]
+        while self.background:
+            self.advance()
+
+
+class Rows:
+    def __init__(self, chains, wide, inner):
+        self.total = sum(chain.rows for chain in chains)
+        self.start = [0]
+        for chain in chains:
+            self.start.append(self.start[-1] + chain.rows)
+        self.mids = 3 * self.total
+        self.wides = self.mids + 8
+        self.shape = (self.wides + 8, wide)
+        self.inner = inner
+
+    def plane(self, place, plane):
+        first = (1 + plane // 2) * self.total + self.start[place]
+        column = plane % 2 * self.inner
+        return first, slice(column, column + self.inner)
+
+
+def classes(units):
+    shapes = []
+    counts = []
+    places = []
+    for unit in units:
+        key = (unit.ways, unit.taps, unit.piece, unit.width)
+        if key not in shapes:
+            shapes.append(key)
+            counts.append(0)
+        index = shapes.index(key)
+        places.append((index, counts[index]))
+        counts[index] += 1
+    return shapes, counts, places
+
+
+def kernel_text(trees, chains, weights, units, sizes, *refs):
     given_tree, made_tree, scratch_tree = trees
     given_size = given_tree.num_leaves
     made_size = made_tree.num_leaves
@@ -1576,82 +1677,100 @@
     made = jax.tree.unflatten(made_tree, refs[given_size : given_size + made_size])
     scratch = jax.tree.unflatten(scratch_tree, refs[given_size + made_size :])
     given = {**given, **dict(chains=[bag(value) for value in given["chains"]])}
-    made = {**made, **dict(chains=[bag(value) for value in made["chains"]])}
     scratch = dict(
         chains=[bag(value) for value in scratch["chains"]],
         weights=[bag(value) for value in scratch["weights"]],
-    )
-    Body(bag(given), bag(made), bag(scratch), chains, weights, sizes).run()
-
-
-def finish_text(chains, weights, sizes, *refs):
+        units=[bag(value) for value in scratch["units"]],
+    )
+    Body(bag(given), bag(made), bag(scratch), chains, weights, units, sizes).run()
+
+
+def finish_text(chains, weights, units, sizes, *refs):
     mid, wide, inner, mpn = sizes
     count = len(weights)
     take = iter(refs)
-    pieces = [next(take) for _ in range(count)]
-    chain_in = [(next(take), next(take)) for _ in chains]
-    mids, wides = next(take), next(take)
+    shapes, _, places = classes(units)
+    layout = Rows(chains, wide, inner)
+    pieces = [next(take) for _ in shapes]
+    rows_in = next(take)
     outs = [next(take) for _ in range(count)]
     groups = [(next(take), next(take)) for _ in range(3)]
     mid_outs = [next(take) for _ in range(8)]
     wide_outs = [next(take) for _ in range(6)]
-    near = [next(take) for _ in range(count)]
+    near = [next(take) for _ in shapes]
+    rows = next(take)
     wided = [next(take) for _ in range(count)]
     woven, came, gone, weave = next(take), next(take), next(take), next(take)
     arrivals = []
-    for index in range(count):
-        copy = pltpu.make_async_copy(pieces[index], near[index], came.at[index])
+    for index, (which, place) in enumerate(places):
+        copy = pltpu.make_async_copy(
+            pieces[which].at[place], near[which].at[place], came.at[index]
+        )
         copy.start()
         arrivals.append(copy)
+    last = pltpu.make_async_copy(rows_in, rows, came.at[len(units)])
+    last.start()
+    leaving = []
+    for index, unit in enumerate(units):
+        arrivals[index].wait()
+        which, place = places[index]
+        width, piece = unit.width, unit.piece
+        stride = weights[unit.tensor].width
+        for core in range(2):
+            for way in range(unit.ways):
+                first = core * (unit.block // 2) + way * piece
+                for source in range(mpn):
+                    column = source * stride + unit.first_column
+                    for tap in range(unit.taps):
+                        wided[unit.tensor][
+                            unit.first_tap + tap,
+                            first : first + piece,
+                            column : column + width,
+                        ] = near[which][place, core, way, source, tap].astype(F32)
+        if index + 1 == len(units) or units[index + 1].tensor != unit.tensor:
+            whole = unit.tensor
+            copy = pltpu.make_async_copy(wided[whole], outs[whole], gone.at[whole])
+            copy.start()
+            leaving.append(copy)
+    last.wait()
     for row, out in enumerate(mid_outs):
-        out[...] = mids[row, :]
+        out[...] = rows[layout.mids + row, :mid]
     for row, out in enumerate(wide_outs):
-        out[...] = wides[row, :]
-    leaving = []
-    for index, weight in enumerate(weights):
-        arrivals[index].wait()
-        width, piece = weight.width, weight.piece
-        for core in range(2):
-            for way in range(weight.ways):
-                first = core * (weight.block // 2) + way * piece
-                for source in range(mpn):
-                    for tap in range(weight.taps):
-                        wided[index][
-                            tap, first : first + piece, source * width : (source + 1) * width
-                        ] = near[index][core, way, source, tap].astype(F32)
-        copy = pltpu.make_async_copy(wided[index], outs[index], gone.at[index])
-        copy.start()
-        leaving.append(copy)
-    for chain, (out_rows, back_rows) in zip(chains, chain_in, strict=True):
+        out[...] = rows[layout.wides + row, :]
+    for place, chain in enumerate(chains):
         for segment in chain.segments:
             out, back = groups[segment.group]
             side = segment.side
-            for i in range(side):
-                if segment.inside:
+            if segment.inside:
+                for i in range(side):
                     for j in range(side):
-                        start = segment.start + i * segment.down + j * segment.right
-                        rows = slice(start, start + segment.images)
-                        out[i, j] = out_rows[rows, :]
+                        offset = segment.start + i * segment.down + j * segment.right
+                        first = layout.start[place] + offset
+                        out[i, j] = rows[first : first + segment.images, :]
                         for plane in range(4):
-                            back[2 * i + plane // 2, 2 * j + plane % 2] = back_rows[
-                                plane, rows, :
+                            first, columns = layout.plane(place, plane)
+                            first += offset
+                            back[2 * i + plane // 2, 2 * j + plane % 2] = rows[
+                                first : first + segment.images, columns
                             ]
-                    continue
-                for image in range(segment.images):
-                    start = segment.start + image * side * side + i * side
-                    rows = slice(start, start + side)
-                    out[image, i] = out_rows[rows, :]
+                continue
+            for image in range(segment.images):
+                for i in range(side):
+                    offset = segment.start + image * side * side + i * side
+                    first = layout.start[place] + offset
+                    out[image, i] = rows[first : first + side, :]
                     for plane in range(4):
+                        first, columns = layout.plane(place, plane)
+                        first += offset
                         for lane in range(inner // LANE):
+                            column = columns.start + lane * LANE
                             woven[
                                 lane,
                                 image,
                                 2 * i + plane // 2,
                                 pl.ds(plane % 2, side, stride=2),
                                 :,
-                            ] = back_rows[plane, rows, lane * LANE : (lane + 1) * LANE]
-            if segment.inside:
-                continue
+                            ] = rows[first : first + side, column : column + LANE]
             for lane in range(inner // LANE):
                 copy = pltpu.make_async_copy(
                     woven.at[lane],
@@ -1709,10 +1828,12 @@
     shapes = [(values.shape[0], values.shape[1]) for values in images]
     chains = [Chain((2, 0), shapes, dpn), Chain((1,), shapes, dpn)]
     weights = weight_table(mid, wide, inner)
+    units = unit_table(weights)
     sizes = (mid, wide, inner, dpn, mpn)
     vmem = pl.BlockSpec(memory_space=VMEM)
     smem = pl.BlockSpec(memory_space=pltpu.SMEM)
     anywhere = pl.BlockSpec(memory_space=pl.ANY)
+    hbm = pl.BlockSpec(memory_space=pltpu.HBM)
 
     def by_tap(spatial):
         return spatial.transpose(1, 2, 0, 3).reshape(9, mid, mpn * mid)
@@ -1749,32 +1870,24 @@
         weights=[anywhere] * WEIGHTS,
     )
     shape = jax.ShapeDtypeStruct
+    layout = Rows(chains, wide, inner)
+    unit_shapes, unit_counts, _ = classes(units)
     made = dict(
-        chains=[
-            dict(
-                out=shape((chain.rows, wide), F32), back=shape((4, chain.rows, inner), F32)
-            )
-            for chain in chains
+        rows=shape(layout.shape, F32),
+        units=[
+            shape((count, 2, ways, mpn, *rest), BF16)
+            for count, (ways, *rest) in zip(unit_counts, unit_shapes, strict=True)
         ],
-        mids=shape((8, mid), F32),
-        wides=shape((8, wide), F32),
-        weights=[
-            shape((2, w.ways, mpn, w.taps, w.piece, w.width), BF16) for w in weights
-        ],
-    )
-    made_specs = dict(
-        chains=[dict(out=vmem, back=vmem) for _ in chains],
-        mids=vmem,
-        wides=vmem,
-        weights=[anywhere] * WEIGHTS,
-    )
+    )
+    made_specs = dict(rows=vmem, units=[anywhere] * len(unit_shapes))
     scratch = dict(
         chains=[chain_scratch(chain, mid, wide, inner, dpn, mpn) for chain in chains],
-        weights=[weight_scratch(weight, dpn, mpn) for weight in weights],
+        weights=[weight_scratch(weight, mpn) for weight in weights],
+        units=[unit_scratch(unit, mpn) for unit in units],
     )
     trees = tuple(jax.tree.structure(tree) for tree in (given_specs, made_specs, scratch))
     results = pl.pallas_call(
-        functools.partial(kernel_text, trees, chains, weights, sizes),
+        functools.partial(kernel_text, trees, chains, weights, units, sizes),
         out_shape=jax.tree.leaves(made),
         in_specs=jax.tree.leaves(given_specs),
         out_specs=jax.tree.leaves(made_specs),
@@ -1799,23 +1912,21 @@
         group_shapes += [laid(s, s.side, wide), laid(s, 2 * s.side, inner)]
     woven = [laid(s, 2 * s.side, inner) for s in segments if not s.inside]
     vector_shapes = [shape((mid,), F32)] * 8 + [shape((wide,), F32)] * 6
-    chain_in = []
-    for value in got.chains:
-        chain_in += [value["out"], value["back"]]
     final = pl.pallas_call(
-        functools.partial(finish_text, chains, weights, (mid, wide, inner, mpn)),
+        functools.partial(finish_text, chains, weights, units, (mid, wide, inner, mpn)),
         out_shape=final_shapes + group_shapes + vector_shapes,
-        in_specs=[anywhere] * WEIGHTS + [vmem] * (len(chain_in) + 2),
-        out_specs=[anywhere] * WEIGHTS
-        + [spec for s in segments for spec in (vmem, vmem if s.inside else anywhere)]
+        in_specs=[hbm] * (len(unit_shapes) + 1),
+        out_specs=[hbm] * WEIGHTS
+        + [spec for s in segments for spec in (vmem, vmem if s.inside else hbm)]
         + [vmem] * len(vector_shapes),
-        scratch_shapes=[VMEM(value.shape, BF16) for value in made["weights"]]
+        scratch_shapes=[VMEM(value.shape, BF16) for value in made["units"]]
+        + [VMEM(layout.shape, F32)]
         + [VMEM(value.shape, F32) for value in final_shapes]
         + [VMEM((inner // LANE, *woven[0].shape[:3], LANE), F32)]
-        + [DMA((WEIGHTS,)), DMA((WEIGHTS,)), DMA((inner // LANE,))],
+        + [DMA((len(units) + 1,)), DMA((WEIGHTS,)), DMA((inner // LANE,))],
         compiler_params=pltpu.CompilerParams(vmem_limit_bytes=48 * 2**20),
         name="finish",
-    )(*got.weights, *chain_in, got.mids, got.wides)
+    )(*got.units, got.rows)
     tensors = final[:WEIGHTS]
     grads = [value[0] for value in tensors]
     for place in (TENSOR_S1, TENSOR_S2):
@@ -1862,7 +1973,7 @@
         and mesh.shape["dp"] == 8
         and mid == LANE
         and inner % LANE == 0
-        and wide % LANE == 0
+        and wide == 2 * inner
     )
 
 

time: 294 us -> 255 us (0.87)
  Pallas kernels: 273 us -> 240 us
  local copies, waits for them, and re-layouts: 16.7 us -> 11.7 us
    pallas_call x2, Pallas kernels: 273 us -> 240 us  [the longest x1 232 us: fused_device(): pl.pallas_call(functools.partial(kernel_text, trees, chains, weights, uni...]
    unnamed x28 -> x12, local copies, waits for them, and re-layouts: 11.1 us -> 5.25 us
where the time goes in v1:
time: 255 us
  Pallas kernels  240 us (94%)
  local copies, waits for them, and re-layouts  11.7 us (5%)
    pallas_call x1, Pallas kernels, fused_device(): pl.pallas_call(functools.partial(kernel_text, trees, chains, weights, uni...  232 us
    pallas_call x1, Pallas kernels, fused_device(): pl.pallas_call(functools.partial(finish_text, chains, weights, units, (mi...  7.62 us
    unnamed x12, local copies, waits for them, and re-layouts  5.25 us

profile of v1, /device:TPU:0, one launch (start us, length us, event | category | flops | bytes accessed | tf_op | source)
XLA Modules:
  0.0 254.9 jit_solution(15478660034029700360)
XLA Ops:
  0.7 0.0 copy-start.5
  1.4 0.8 reshape_transpose.6
  2.2 0.9 reshape_transpose.7
  3.2 1.0 reshape.87
  4.2 0.0 copy-start.4
  4.2 0.7 fusion.5.refs_0_
  4.9 1.0 reshape.91
  6.0 0.7 pad.28.refs_3_
  6.7 0.0 copy-done.5
  6.7 0.1 copy.72
  6.8 0.1 reshape.89
  6.9 0.8 fusion.2.refs_2_
  7.7 0.0 copy-done.4
  7.7 0.3 reshape.92
  8.1 0.3 copy.71
  8.4 0.2 reshape.93
  8.6 0.1 copy.67
  8.7 0.8 pad.29.refs_5_
  9.5 232.3 %bottlenecks.1 = (f32[1408,512]{1,0:T(8,128)}, bf16[3,2,2,4,1,32,512]{6,5,4,3,2,1,0:T(8,128)(2,1)}, bf16[6,2,2,4,3,32,128]{6,5,4,3,2,1,0:T(8,128)(2,1)}, bf16[2,...) custom-call(bf16[240,512]{1,0:T(8,128)(2,1)} %fusion.5.refs_0_, ...), custom_call_target="tpu_custom_call" | custom-call | tf_op jit(solution)/shard_map/bottlenecks/pallas_call | solution.py:1889
  241.8 0.0 copy-start
  241.8 1.7 copy-done
  243.5 0.0 copy-start.1
  243.5 1.4 copy-done.1
  244.9 0.0 copy-start.2
  244.9 1.2 copy-done.2
  246.1 0.0 copy-start.3
  246.1 0.9 copy-done.3
  247.1 7.6 %finish.1 = (f32[1,128,1024]{2,1,0:T(8,128)}, f32[9,128,512]{2,1,0:T(8,128)}, f32[1,128,2048]{2,1,0:T(8,128)}, f32[1,256,2048]{2,1,0:T(8,128)}, f32[1,128,2048]{...) custom-call(bf16[3,2,2,4,1,32,512]{6,5,4,3,2,1,0:T(8,128)(2,1)S(1)} , ...), custom_call_target="tpu_custom_call" | custom-call | tf_op jit(solution)/shard_map/finish/pallas_call | solution.py:1915
  (3 shorter events, 0.1 us)
Async XLA Ops:
  0.7 6.0 %copy-start.5 = (bf16[4,14,14,256]{3,0,2,1:T(4,128)(2,1)S(1)}, bf16[4,14,14,256]{3,0,2,1:T(4,128)(2,1)}, u32[]{:S(2)}) copy-start(bf16[4,14,14,256]{3,0,2,1:T(4,128)(2,1)} %param.35) | copy-start | bytes 1204228
  4.2 3.5 %copy-start.4 = (bf16[6,12,12,256]{3,2,1,0:T(8,128)(2,1)S(1)}, bf16[6,12,12,256]{3,2,1,0:T(8,128)(2,1)}, u32[]{:S(2)}) copy-start(bf16[6,12,12,256]{3,2,1,0:T(8,128)(2,1)} %param.34) | copy-start | bytes 1327108
  241.8 1.7 copy-start
  243.5 1.4 copy-start.1
  244.9 1.2 copy-start.2
  246.1 0.9 copy-start.3

commit v2 on v1

--- a/solution.py
+++ b/solution.py
@@ -717,6 +717,7 @@
         dt=VMEM((padded, 9 * mid), F32),
         d=VMEM((4, rows, mid), F32),
         back=VMEM((rows, inner), F32),
+        late=DMA((2,)),
         gate=VMEM((rows, LANE), F32),
         facm=VMEM((4, 8, mid), F32),
         facw=VMEM((3, 8, wide), F32),
@@ -1148,6 +1149,26 @@
                     start = segment.start + image * area
                     link.gate[start : start + area, :] = jnp.full((area, LANE), flag, F32)
 
+    def lay_cotangent(self, chain, link):
+        for segment in chain.segments:
+            source = self.given.cotangents[segment.group]
+            side = segment.side
+            whole = segment.start + segment.real // 8 * 8
+            if whole < segment.stop:
+                link.d2[whole : segment.stop, :] = jnp.zeros(
+                    (segment.stop - whole, self.wide), F32
+                )
+            if segment.inside:
+                for i in range(side):
+                    for j in range(side):
+                        first = segment.start + i * segment.down + j * segment.right
+                        link.d2[first : first + segment.images, :] = source[i, j].astype(F32)
+            else:
+                for image in range(segment.images):
+                    for i in range(side):
+                        first = segment.start + (image * side + i) * side
+                        link.d2[first : first + side, :] = source[image, i].astype(F32)
+
     def gates(self, link, rows):
         return jnp.concatenate([link.gate[rows, :]] * (self.wide // LANE), axis=1)
 
@@ -1252,7 +1273,7 @@
             logistic = jax.nn.sigmoid(final)
             self.made.rows[start + segment.start : start + segment.stop, :] = final * logistic
             slope = logistic * (1.0 + final * (1.0 - logistic))
-            change = slope * given.cotangent[span, :].astype(F32)
+            change = slope * link.d2[span, :]
             link.d2[span, :] = change
             gated = gate * change
             terms.append(self.sum_rows(gated))
@@ -1347,14 +1368,29 @@
                 link.k1.full[self.mp, start : start + segment.size, :] = values[plane]
 
         self.narrow_back(chain, link, NORM_Q1, link.d, totals, link.n1, store_back_one)
-        yield from self.gather(link.k1)
-        product = nn(self.joined(link.k1), self.weight(TENSOR_Q1))
-        for plane in range(4):
-            first, columns = self.rows.plane(place, plane)
-            values = product[plane * rows : (plane + 1) * rows, :]
-            if plane == 0:
-                values = values + link.back[...]
-            self.made.rows[first : first + rows, columns] = values
+        span = 2 * rows
+        for part in range(3):
+            if part < 2:
+                mine = link.k1.full.at[self.mp, part * span : (part + 1) * span]
+                sems = link.k1.sems if part == 0 else link.late
+                for peer in self.peers:
+                    self.remote(mine, mine, sems.at[0], sems.at[1], (self.dp, peer)).start()
+            if part > 0:
+                before = slice((part - 1) * span, part * span)
+                full = link.k1.full
+                pixels = jnp.concatenate([full[k, before] for k in range(self.mpn)], axis=1)
+                product = nn(pixels, self.weight(TENSOR_Q1))
+                for half in range(2):
+                    plane = 2 * (part - 1) + half
+                    first, columns = self.rows.plane(place, plane)
+                    values = product[half * rows : (half + 1) * rows, :]
+                    if plane == 0:
+                        values = values + link.back[...]
+                    self.made.rows[first : first + rows, columns] = values
+            if part < 2:
+                yield
+                slab = link.k1.full.at[0 : self.mpn - 1, part * span : (part + 1) * span]
+                self.settle(slab, sems, (self.dp, self.peers[0]))
 
     def bypass_back(self, link):
         product = nt(link.dzp[...], self.weight(TENSOR_SC))
@@ -1541,8 +1577,8 @@
                 cast(way, backward(way)).wait_send()
 
 
-    def launch(self, task):
-        self.background.append([task, 0])
+    def launch(self, task, delay=0):
+        self.background.append([task, delay])
 
     def advance(self):
         for entry in list(self.background):
@@ -1580,17 +1616,28 @@
 
         def grad(tensor, part=0):
             places = [place for place, unit in enumerate(self.units) if unit.tensor == tensor]
-            return lambda: self.launch(self.unit_gradient(places[part]))
+            return lambda: self.launch(self.unit_gradient(places[part]), part)
 
         def bypass(index):
             chain, link, given, _ = parts[index]
             return lambda: self.launch(self.bypass(chain, link, given.pixels))
 
+        def cotangent(index):
+            chain, link, _, _ = parts[index]
+            return lambda: self.lay_cotangent(chain, link)
+
         def bypass_back(index):
             return lambda: self.launch(self.bypass_back(self.links[index]))
 
         events = {
-            1: (lift(TENSOR_S1), lift(TENSOR_E1), lift(TENSOR_SC), lift(TENSOR_Q2)),
+            1: (
+                lift(TENSOR_S1),
+                lift(TENSOR_E1),
+                lift(TENSOR_SC),
+                lift(TENSOR_Q2),
+                cotangent(0),
+                cotangent(1),
+            ),
             2: (bypass(0), start(TENSOR_S2), start(TENSOR_E2), hand(TENSOR_S1)),
             3: (lift(TENSOR_S2, (0, 1)),),
             4: (bypass(1), hand(TENSOR_E1), hand(TENSOR_SC)),
@@ -1603,9 +1650,8 @@
             17: (grad(TENSOR_S2, 0),),
             18: (grad(TENSOR_S2, 1),),
             19: (grad(TENSOR_S2, 2), grad(TENSOR_Q2)),
-            20: (grad(TENSOR_E1),),
-            21: (bypass_back(0), grad(TENSOR_SC, 0)),
-            22: (grad(TENSOR_SC, 1),),
+            20: (grad(TENSOR_E1), grad(TENSOR_SC, 0)),
+            21: (bypass_back(0), grad(TENSOR_SC, 1)),
             23: (
                 bypass_back(1),
                 grad(TENSOR_S1, 0),
@@ -1616,16 +1662,14 @@
         slot = 0
         while tasks:
             slot += 1
+            rounds = (0, 2) if slot in (24, 25) else (1, 1)
             for place, task in enumerate(list(tasks)):
                 if next(task, self) is self:
                     tasks.remove(task)
-                if place == 0:
-                    self.advance()
-            for event in events.get(slot, ()):
-                event()
-            self.advance()
-            if slot == 24:
-                for _ in range(8):
+                if place == 1:
+                    for event in events.get(slot, ()):
+                        event()
+                for _ in range(rounds[place]):
                     self.advance()
         self.launch(self.unit_gradient(len(self.units) - 1))
         self.advance()
@@ -1845,12 +1889,6 @@
         chains=[
             dict(
                 pixels=rows_of(chain, lambda s: planes_of(s, images[s.group])),
-                cotangent=rows_of(
-                    chain,
-                    lambda s: padded_rows(
-                        s.pixel_first(cotangents[s.group]).reshape(s.real, wide), s.size
-                    ),
-                ),
                 edges=edge_masks(chain),
             )
             for chain in chains
@@ -1859,14 +1897,21 @@
         wides=wides,
         widths=widths,
         gates=list(gates),
+        cotangents=[
+            s.pixel_first(cotangents[s.group])
+            for s in sorted(
+                (s for chain in chains for s in chain.segments), key=lambda s: s.group
+            )
+        ],
         weights=[q1[None], by_tap(s1), e1[None], sc[None], q2[None], by_tap(s2), e2[None]],
     )
     given_specs = dict(
-        chains=[dict(pixels=vmem, cotangent=vmem, edges=vmem) for _ in chains],
+        chains=[dict(pixels=vmem, edges=vmem) for _ in chains],
         mids=[vmem] * len(mids),
         wides=[vmem] * len(wides),
         widths=smem,
         gates=[smem] * 3,
+        cotangents=[vmem] * 3,
         weights=[anywhere] * WEIGHTS,
     )
     shape = jax.ShapeDtypeStruct
@@ -1924,7 +1969,7 @@
         + [VMEM(value.shape, F32) for value in final_shapes]
         + [VMEM((inner // LANE, *woven[0].shape[:3], LANE), F32)]
         + [DMA((len(units) + 1,)), DMA((WEIGHTS,)), DMA((inner // LANE,))],
-        compiler_params=pltpu.CompilerParams(vmem_limit_bytes=48 * 2**20),
+        compiler_params=pltpu.CompilerParams(vmem_limit_bytes=62 * 2**20),
         name="finish",
     )(*got.units, got.rows)
     tensors = final[:WEIGHTS]

time: 255 us -> 241 us (0.945)
  Pallas kernels: 240 us -> 233 us
  local copies, waits for them, and re-layouts: 11.7 us -> 5.41 us
    pallas_call x1, Pallas kernels: 232 us -> 224 us  [fused_device(): pl.pallas_call(functools.partial(kernel_text, trees, chains, weights, uni...]
    unnamed x12 -> x2, local copies, waits for them, and re-layouts: 5.25 us -> 0.01 us
where the time goes in v2:
time: 241 us
  Pallas kernels  233 us (97%)
  local copies, waits for them, and re-layouts  5.41 us (2%)
    pallas_call x1, Pallas kernels, fused_device(): pl.pallas_call(functools.partial(kernel_text, trees, chains, weights, uni...  224 us
    pallas_call x1, Pallas kernels, fused_device(): pl.pallas_call(functools.partial(finish_text, chains, weights, units, (mi...  9.13 us

profile of v2, /device:TPU:0, one launch (start us, length us, event | category | flops | bytes accessed | tf_op | source)
XLA Modules:
  0.0 240.8 jit_solution(15136825085980261607)
XLA Ops:
  0.7 0.0 copy-start
  1.4 0.9 reshape_transpose.3
  2.4 1.4 copy.68.refs_4_
  3.9 1.1 copy.73
  5.0 0.1 reshape.82
  5.1 0.8 fusion.2.refs_1_
  5.9 0.0 copy-done
  5.9 0.3 reshape.84
  6.3 0.3 copy.72
  6.6 0.2 reshape.85
  6.8 0.1 copy.67
  6.9 0.8 pad.14.refs_3_
  7.7 223.8 %bottlenecks.1 = (f32[1408,512]{1,0:T(8,128)}, bf16[3,2,2,4,1,32,512]{6,5,4,3,2,1,0:T(8,128)(2,1)}, bf16[6,2,2,4,3,32,128]{6,5,4,3,2,1,0:T(8,128)(2,1)}, bf16[2,...) custom-call(f32[2,4,304,128]{3,2,1,0:T(8,128)} %constant.7.clone.refs_0_, ...), custom_call_target="tpu_custom_call" | custom-call | tf_op jit(solution)/shard_map/bottlenecks/pallas_call | solution.py:1934
  231.5 9.1 %finish.1 = (f32[1,128,1024]{2,1,0:T(8,128)}, f32[9,128,512]{2,1,0:T(8,128)}, f32[1,128,2048]{2,1,0:T(8,128)}, f32[1,256,2048]{2,1,0:T(8,128)}, f32[1,128,2048]{...) custom-call(bf16[3,2,2,4,1,32,512]{6,5,4,3,2,1,0:T(8,128)(2,1)} %get, ...), custom_call_target="tpu_custom_call" | custom-call | tf_op jit(solution)/shard_map/finish/pallas_call | solution.py:1960
  (3 shorter events, 0.1 us)
Async XLA Ops:
  0.7 5.2 %copy-start = (bf16[6,12,12,256]{3,2,1,0:T(8,128)(2,1)S(1)}, bf16[6,12,12,256]{3,2,1,0:T(8,128)(2,1)}, u32[]{:S(2)}) copy-start(bf16[6,12,12,256]{3,2,1,0:T(8,128)(2,1)} %param.34) | copy-start | bytes 1327108

commit v3 on v2

--- a/solution.py
+++ b/solution.py
@@ -717,6 +717,9 @@
         dt=VMEM((padded, 9 * mid), F32),
         d=VMEM((4, rows, mid), F32),
         back=VMEM((rows, inner), F32),
+        pixels=VMEM((4, rows, inner), BF16),
+        edges=VMEM((len(chain.segments), 4, padded, LANE), F32),
+        loads=DMA((2,)),
         late=DMA((2,)),
         gate=VMEM((rows, LANE), F32),
         facm=VMEM((4, 8, mid), F32),
@@ -768,6 +771,8 @@
         self.places = classes(units)[2]
         self.rows = Rows(chains, sizes[1], sizes[2])
         self.sums = scratch.units
+        self.result = scratch.rows
+        self.result_sem = scratch.rows_out
         self.chains = chains
         self.mid, self.wide, self.inner, self.dpn, self.mpn = sizes
         self.dp = lax.axis_index("dp")
@@ -1271,7 +1276,7 @@
                 normed * self.wide_row(NORM_E2, 0) + self.wide_row(NORM_E2, 1)
             )
             logistic = jax.nn.sigmoid(final)
-            self.made.rows[start + segment.start : start + segment.stop, :] = final * logistic
+            self.result[start + segment.start : start + segment.stop, :] = final * logistic
             slope = logistic * (1.0 + final * (1.0 - logistic))
             change = slope * link.d2[span, :]
             link.d2[span, :] = change
@@ -1386,7 +1391,7 @@
                     values = product[half * rows : (half + 1) * rows, :]
                     if plane == 0:
                         values = values + link.back[...]
-                    self.made.rows[first : first + rows, columns] = values
+                    self.result[first : first + rows, columns] = values
             if part < 2:
                 yield
                 slab = link.k1.full.at[0 : self.mpn - 1, part * span : (part + 1) * span]
@@ -1400,9 +1405,9 @@
 
     def unit_product(self, unit):
         total = None
-        for link, given in zip(self.links, self.given.chains, strict=True):
+        for link in self.links:
             if unit.tensor == TENSOR_Q1:
-                pixels = given.pixels[...]
+                pixels = link.pixels[...]
                 part = tn(self.joined(link.k1), pixels.reshape(-1, self.inner))
             else:
                 left, right = {
@@ -1592,16 +1597,24 @@
                 entry[1] = pause or 1
 
     def run(self):
+        loads = []
+        for link, given in zip(self.links, self.given.chains, strict=True):
+            loads.append(
+                pltpu.make_async_copy(given.pixels, link.pixels, link.loads.at[0])
+            )
+            loads.append(pltpu.make_async_copy(given.edges, link.edges, link.loads.at[1]))
+        for load in loads:
+            load.start()
         self.barrier()
         for tensor in (TENSOR_Q1, TENSOR_S1, TENSOR_E1, TENSOR_SC, TENSOR_Q2):
             self.weight_start(tensor)
         for chain, link in zip(self.chains, self.links, strict=True):
             self.clear(chain, link)
+        for load in loads:
+            load.wait()
         parts = [
-            (chain, link, given, place)
-            for place, (chain, link, given) in enumerate(
-                zip(self.chains, self.links, self.given.chains, strict=True)
-            )
+            (chain, link, link, place)
+            for place, (chain, link) in enumerate(zip(self.chains, self.links, strict=True))
         ]
         tasks = [self.chain(*part) for part in parts]
 
@@ -1675,10 +1688,13 @@
         self.advance()
         first, second = self.links
         mids, wides = self.rows.mids, self.rows.wides
-        self.made.rows[mids : mids + 8, : self.mid] = first.gm[...] + second.gm[...]
-        self.made.rows[wides : wides + 8, :] = first.gw[...] + second.gw[...]
+        self.result[mids : mids + 8, : self.mid] = first.gm[...] + second.gm[...]
+        self.result[wides : wides + 8, :] = first.gw[...] + second.gw[...]
+        leaving = pltpu.make_async_copy(self.result, self.made.rows, self.result_sem.at[0])
+        leaving.start()
         while self.background:
             self.advance()
+        leaving.wait()
 
 
 class Rows:
@@ -1725,6 +1741,8 @@
         chains=[bag(value) for value in scratch["chains"]],
         weights=[bag(value) for value in scratch["weights"]],
         units=[bag(value) for value in scratch["units"]],
+        rows=scratch["rows"],
+        rows_out=scratch["rows_out"],
     )
     Body(bag(given), bag(made), bag(scratch), chains, weights, units, sizes).run()
 
@@ -1906,7 +1924,7 @@
         weights=[q1[None], by_tap(s1), e1[None], sc[None], q2[None], by_tap(s2), e2[None]],
     )
     given_specs = dict(
-        chains=[dict(pixels=vmem, edges=vmem) for _ in chains],
+        chains=[dict(pixels=anywhere, edges=anywhere) for _ in chains],
         mids=[vmem] * len(mids),
         wides=[vmem] * len(wides),
         widths=smem,
@@ -1924,11 +1942,13 @@
             for count, (ways, *rest) in zip(unit_counts, unit_shapes, strict=True)
         ],
     )
-    made_specs = dict(rows=vmem, units=[anywhere] * len(unit_shapes))
+    made_specs = dict(rows=anywhere, units=[anywhere] * len(unit_shapes))
     scratch = dict(
         chains=[chain_scratch(chain, mid, wide, inner, dpn, mpn) for chain in chains],
         weights=[weight_scratch(weight, mpn) for weight in weights],
         units=[unit_scratch(unit, mpn) for unit in units],
+        rows=VMEM(layout.shape, F32),
+        rows_out=DMA((1,)),
     )
     trees = tuple(jax.tree.structure(tree) for tree in (given_specs, made_specs, scratch))
     results = pl.pallas_call(

time: 241 us -> 239 us (level)
  no operation moved by 1% of the time
where the time goes in v3:
time: 239 us; the launch traced here: 238 us
  Pallas kernels  231 us (97%)
  local copies, waits for them, and re-layouts  5.41 us (2%)
    pallas_call x1, Pallas kernels, fused_device(): pl.pallas_call(functools.partial(kernel_text, trees, chains, weights, uni...  221 us
    pallas_call x1, Pallas kernels, fused_device(): pl.pallas_call(functools.partial(finish_text, chains, weights, units, (mi...  9.13 us

profile of v3, /device:TPU:0, one launch (start us, length us, event | category | flops | bytes accessed | tf_op | source)
XLA Modules:
  0.0 238.5 jit_solution(7247243421271883517)
XLA Ops:
  0.7 0.0 copy-start
  1.4 0.9 reshape_transpose.3
  2.4 1.4 copy.68.refs_4_
  3.9 1.1 copy.73
  5.0 0.1 reshape.82
  5.1 0.8 fusion.2.refs_1_
  5.9 0.0 copy-done
  5.9 0.3 reshape.84
  6.3 0.3 copy.72
  6.6 0.2 reshape.85
  6.8 0.1 copy.67
  6.9 0.8 pad.14.refs_3_
  7.7 221.5 %bottlenecks.1 = (f32[1408,512]{1,0:T(8,128)}, bf16[3,2,2,4,1,32,512]{6,5,4,3,2,1,0:T(8,128)(2,1)}, bf16[6,2,2,4,3,32,128]{6,5,4,3,2,1,0:T(8,128)(2,1)}, bf16[2,...) custom-call(f32[2,4,304,128]{3,2,1,0:T(8,128)} %constant.7.clone.refs_0_, ...), custom_call_target="tpu_custom_call" | custom-call | tf_op jit(solution)/shard_map/bottlenecks/pallas_call | solution.py:1954
  229.2 9.1 %finish.1 = (f32[1,128,1024]{2,1,0:T(8,128)}, f32[9,128,512]{2,1,0:T(8,128)}, f32[1,128,2048]{2,1,0:T(8,128)}, f32[1,256,2048]{2,1,0:T(8,128)}, f32[1,128,2048]{...) custom-call(bf16[3,2,2,4,1,32,512]{6,5,4,3,2,1,0:T(8,128)(2,1)} %get, ...), custom_call_target="tpu_custom_call" | custom-call | tf_op jit(solution)/shard_map/finish/pallas_call | solution.py:1980
  (3 shorter events, 0.1 us)
Async XLA Ops:
  0.7 5.2 %copy-start = (bf16[6,12,12,256]{3,2,1,0:T(8,128)(2,1)S(1)}, bf16[6,12,12,256]{3,2,1,0:T(8,128)(2,1)}, u32[]{:S(2)}) copy-start(bf16[6,12,12,256]{3,2,1,0:T(8,128)(2,1)} %param.34) | copy-start | bytes 1327108
